TPU v7x, 32 devices: a whole 2x2x4 slice. The times are simulated.
32 devices in a mesh: nodes: 8 (over z, x), cols: 4 (over y, core).
Axes of the slice: x: 2, y: 2, z: 4, core: 2. Of those that a mesh axis runs over, the one named last changes fastest.
Arguments:
- node_feats: bfloat16 [8192, 256], P(('nodes', 'cols')), may hold values from -6 to 6
- tile_row: int32 [8, 1408], P('nodes', 'cols'), may hold values from 0 to 7, as said below
- tile_col: int32 [8, 1408], P('nodes', 'cols'), may hold values from 0 to 15
- tile_bits: int32 [8, 1408, 16, 128], P('nodes', 'cols'), may hold values from 0 to 255, as said below
- w_self: bfloat16 [256, 256], replicated, may hold values from -0.375 to 0.375
- w_neigh: bfloat16 [256, 256], replicated, may hold values from -1.5 to 1.5
- bias: float32 [256], replicated, may hold values from -3 to 3
- cotangent: bfloat16 [8192, 256], P(('nodes', 'cols')), may hold values from -6 to 6
Outputs:
- layer_out: bfloat16 [8192, 256], P(('nodes', 'cols'))
- feat_grad: bfloat16 [8192, 256], P(('nodes', 'cols'))
- self_grad: float32 [256, 256], replicated
- neigh_grad: float32 [256, 256], replicated
- bias_grad: float32 [256], replicated
Inputs may be any that keep to these rules, and one draw needn't show every extreme that they name: `tile_row`: destination row block of a tile within its nodes group; in every nodes group at least one block carries no tile. `tile_col`: source row block of a tile within its cols index; a block may carry several tiles. `tile_bits`: bit j of word (w, a) of a tile is its edge from destination row a to source column 8 w + j; bits above the eighth are zero; some destination rows have no edge in any tile.
All inputs are finite; a program needn't handle non-finite values.
Results may differ from a plain program's by a relative error of at most 0.0075.
Values may be sent and summed in bfloat16 or wider, within the bound.
A program may use at most 64 MiB of HBM per device.

v0:
```python
import math

import jax
import jax.numpy as jnp
from jax import lax
from jax.sharding import PartitionSpec as P


def unpack_tiles(packed):
    shifts = jnp.arange(8, dtype=jnp.int32)
    edge_flags = jnp.right_shift(packed[:, :, None, :], shifts[None, None, :, None]) & 1
    return edge_flags.reshape(packed.shape[0], 128, 128)


def shards(node_feats, tile_row, tile_col, tile_bits, w_self, w_neigh, bias, cotangent):
    rows_dev = node_feats.shape[0]
    width_in = node_feats.shape[1]
    node_count = lax.axis_size("nodes")
    col_count = lax.axis_size("cols")
    per_dev = rows_dev // 128
    dest_count = col_count * per_dev
    source_count = node_count * per_dev
    tile_count = tile_row.shape[1]
    tile_group = math.gcd(tile_count, 32)
    group_count = tile_count // tile_group
    rows_here = tile_row[0].reshape(group_count, tile_group)
    cols_here = tile_col[0].reshape(group_count, tile_group)
    packed_here = tile_bits[0].reshape(group_count, tile_group, 16, 128)
    source = lax.all_gather(node_feats, "nodes", axis=0, tiled=True)
    source_blocks = source.reshape(source_count, 128, width_in)

    def forward_step(totals, tile_set):
        summed, degree = totals
        rows_blk, cols_blk, packed_blk = tile_set
        edge_flags = unpack_tiles(packed_blk)
        bits_blk = edge_flags.astype(jnp.bfloat16)
        picked = source_blocks[cols_blk]
        products = jnp.einsum("tba,tbf->taf", bits_blk, picked, preferred_element_type=jnp.float32)
        summed = summed.at[rows_blk].add(products)
        degree = degree.at[rows_blk].add(jnp.sum(edge_flags, axis=1).astype(jnp.float32))
        return ((summed, degree), None)

    initial = (
        jnp.zeros((dest_count, 128, width_in), jnp.float32),
        jnp.zeros((dest_count, 128), jnp.float32),
    )
    (partial_sum, degree_part), _ = lax.scan(
        forward_step, initial, (rows_here, cols_here, packed_here)
    )
    summed, degree = (
        lax.psum_scatter(
            partial_sum.reshape(dest_count * 128, width_in), "cols", scatter_dimension=0, tiled=True
        ),
        lax.psum_scatter(
            degree_part.reshape(dest_count * 128), "cols", scatter_dimension=0, tiled=True
        ),
    )
    degree = jnp.maximum(degree, 1.0)
    neigh_mean = (summed / degree[:, None]).astype(jnp.bfloat16)
    preact = (
        jnp.dot(node_feats, w_self, preferred_element_type=jnp.float32)
        + jnp.dot(neigh_mean, w_neigh, preferred_element_type=jnp.float32)
        + bias
    )
    sigmoid_pre = jax.nn.sigmoid(preact)
    layer_out = (preact * sigmoid_pre).astype(jnp.bfloat16)
    pre_grad = (
        cotangent.astype(jnp.float32) * sigmoid_pre * (1.0 + preact * (1.0 - sigmoid_pre))
    ).astype(jnp.bfloat16)
    self_term = jnp.dot(node_feats.T, pre_grad, preferred_element_type=jnp.float32)
    neigh_term = jnp.dot(neigh_mean.T, pre_grad, preferred_element_type=jnp.float32)
    bias_term = jnp.sum(pre_grad.astype(jnp.float32), axis=0)
    self_grad, neigh_grad, bias_grad = lax.psum(
        (self_term, neigh_term, bias_term), ("nodes", "cols")
    )
    mean_grad = (
        jnp.dot(pre_grad, w_neigh.T, preferred_element_type=jnp.float32) / degree[:, None]
    ).astype(jnp.bfloat16)
    dest_grad = lax.all_gather(mean_grad, "cols", axis=0, tiled=True)
    grad_blocks = dest_grad.reshape(dest_count, 128, width_in)

    def backward_step(src_grad, tile_set):
        rows_blk, cols_blk, packed_blk = tile_set
        bits_blk = unpack_tiles(packed_blk).astype(jnp.bfloat16)
        picked = grad_blocks[rows_blk]
        products = jnp.einsum("tba,taf->tbf", bits_blk, picked, preferred_element_type=jnp.float32)
        return (src_grad.at[cols_blk].add(products), None)

    src_total, _ = lax.scan(
        backward_step,
        jnp.zeros((source_count, 128, width_in), jnp.float32),
        (rows_here, cols_here, packed_here),
    )
    src_total = src_total.reshape(source_count * 128, width_in)
    src_grad = lax.psum_scatter(src_total, "nodes", scatter_dimension=0, tiled=True)
    feat_grad = (jnp.dot(pre_grad, w_self.T, preferred_element_type=jnp.float32) + src_grad).astype(
        jnp.bfloat16
    )
    return (layer_out, feat_grad, self_grad, neigh_grad, bias_grad)


def solution(mesh):
    return jax.shard_map(
        shards,
        mesh=mesh,
        in_specs=(
            P(("nodes", "cols"), None),
            P("nodes", "cols"),
            P("nodes", "cols"),
            P("nodes", "cols", None, None),
            P(),
            P(),
            P(),
            P(("nodes", "cols"), None),
        ),
        out_specs=(P(("nodes", "cols"), None), P(("nodes", "cols"), None), P(), P(), P()),
        check_vma=False,
    )
```

profile of v0, /device:TPU:1, one launch (start us, length us, event | category | flops | bytes accessed | tf_op | source)
XLA Modules:
  0.0 487.4 jit_solution(10082361201258682326)
XLA Ops:
  10.1 41.3 %all-gather.2.cloned.1.call-done = bf16[2048,256]{1,0:T(8,128)(2,1)} async-done(((bf16[256,256]{1,0:T(8,128)(2,1)}), bf16[2048,256]{1,0:T(8,128)(2,1)}) %all-gather.2.cloned.1.call-update) | async-done | bytes 1048592 | tf_op jit(solution)/shard_map/all_gather | solution.py:29
  52.1 159.4 %while.22 = (s32[]{:T(128)}, f32[8,128,256]{2,1,0:T(8,128)S(1)}, f32[8,128]{1,0:T(8,128)}, s32[11,32]{1,0:T(8,128)S(1)}, s32[11,32,16,128]{3,2,1,0:T(8,128)}, /*...) while((s32[]{:T(128)}, f32[8,128,256]{2,1,0:T(8,128)S(1)}, f32[8,128]{1,0:T(8,128)}, ...), condition=%wide.region_4.5_spmd, body=%wide.region_0.4_spmd.sunk | while | flops 272635072 | bytes 24194076 | solution.py:47
  58.6 6.4 %scatter_fusion = f32[8,128,256]{2,1,0:T(8,128)S(1)} fusion(f32[8,128,256]{2,1,0:T(8,128)S(1)} %get-tuple-element.232, s32[32]{0:T(128)S(1)} %get-tuple-element.213, f32[32,128,256]{2,1,0:T(8,128)} %fusion.56), kind=kCustom, calls=%fused_computation.2.clone.1 | custom fusion | flops 1048576 | bytes 12583040 | tf_op jit(solution)/shard_map/while/body/eval_jaxpr/scatter-add | solution.py:39
  70.3 2.8 fusion.56
  73.0 6.4 %scatter_fusion = f32[8,128,256]{2,1,0:T(8,128)S(1)} fusion(f32[8,128,256]{2,1,0:T(8,128)S(1)} %get-tuple-element.232, s32[32]{0:T(128)S(1)} %get-tuple-element.213, f32[32,128,256]{2,1,0:T(8,128)} %fusion.56), kind=kCustom, calls=%fused_computation.2.clone.1 | custom fusion | flops 1048576 | bytes 12583040 | tf_op jit(solution)/shard_map/while/body/eval_jaxpr/scatter-add | solution.py:39
  84.8 2.8 fusion.56
  87.5 6.4 %scatter_fusion = f32[8,128,256]{2,1,0:T(8,128)S(1)} fusion(f32[8,128,256]{2,1,0:T(8,128)S(1)} %get-tuple-element.232, s32[32]{0:T(128)S(1)} %get-tuple-element.213, f32[32,128,256]{2,1,0:T(8,128)} %fusion.56), kind=kCustom, calls=%fused_computation.2.clone.1 | custom fusion | flops 1048576 | bytes 12583040 | tf_op jit(solution)/shard_map/while/body/eval_jaxpr/scatter-add | solution.py:39
  102.0 6.4 %scatter_fusion = f32[8,128,256]{2,1,0:T(8,128)S(1)} fusion(f32[8,128,256]{2,1,0:T(8,128)S(1)} %get-tuple-element.232, s32[32]{0:T(128)S(1)} %get-tuple-element.213, f32[32,128,256]{2,1,0:T(8,128)} %fusion.56), kind=kCustom, calls=%fused_computation.2.clone.1 | custom fusion | flops 1048576 | bytes 12583040 | tf_op jit(solution)/shard_map/while/body/eval_jaxpr/scatter-add | solution.py:39
  113.7 2.8 fusion.56
  116.5 6.4 %scatter_fusion = f32[8,128,256]{2,1,0:T(8,128)S(1)} fusion(f32[8,128,256]{2,1,0:T(8,128)S(1)} %get-tuple-element.232, s32[32]{0:T(128)S(1)} %get-tuple-element.213, f32[32,128,256]{2,1,0:T(8,128)} %fusion.56), kind=kCustom, calls=%fused_computation.2.clone.1 | custom fusion | flops 1048576 | bytes 12583040 | tf_op jit(solution)/shard_map/while/body/eval_jaxpr/scatter-add | solution.py:39
  128.2 2.8 fusion.56
  131.0 6.4 %scatter_fusion = f32[8,128,256]{2,1,0:T(8,128)S(1)} fusion(f32[8,128,256]{2,1,0:T(8,128)S(1)} %get-tuple-element.232, s32[32]{0:T(128)S(1)} %get-tuple-element.213, f32[32,128,256]{2,1,0:T(8,128)} %fusion.56), kind=kCustom, calls=%fused_computation.2.clone.1 | custom fusion | flops 1048576 | bytes 12583040 | tf_op jit(solution)/shard_map/while/body/eval_jaxpr/scatter-add | solution.py:39
  142.7 2.8 fusion.56
  145.5 6.4 %scatter_fusion = f32[8,128,256]{2,1,0:T(8,128)S(1)} fusion(f32[8,128,256]{2,1,0:T(8,128)S(1)} %get-tuple-element.232, s32[32]{0:T(128)S(1)} %get-tuple-element.213, f32[32,128,256]{2,1,0:T(8,128)} %fusion.56), kind=kCustom, calls=%fused_computation.2.clone.1 | custom fusion | flops 1048576 | bytes 12583040 | tf_op jit(solution)/shard_map/while/body/eval_jaxpr/scatter-add | solution.py:39
  157.2 2.8 fusion.56
  160.0 6.4 %scatter_fusion = f32[8,128,256]{2,1,0:T(8,128)S(1)} fusion(f32[8,128,256]{2,1,0:T(8,128)S(1)} %get-tuple-element.232, s32[32]{0:T(128)S(1)} %get-tuple-element.213, f32[32,128,256]{2,1,0:T(8,128)} %fusion.56), kind=kCustom, calls=%fused_computation.2.clone.1 | custom fusion | flops 1048576 | bytes 12583040 | tf_op jit(solution)/shard_map/while/body/eval_jaxpr/scatter-add | solution.py:39
  174.5 6.4 %scatter_fusion = f32[8,128,256]{2,1,0:T(8,128)S(1)} fusion(f32[8,128,256]{2,1,0:T(8,128)S(1)} %get-tuple-element.232, s32[32]{0:T(128)S(1)} %get-tuple-element.213, f32[32,128,256]{2,1,0:T(8,128)} %fusion.56), kind=kCustom, calls=%fused_computation.2.clone.1 | custom fusion | flops 1048576 | bytes 12583040 | tf_op jit(solution)/shard_map/while/body/eval_jaxpr/scatter-add | solution.py:39
  186.2 2.8 fusion.56
  189.0 6.4 %scatter_fusion = f32[8,128,256]{2,1,0:T(8,128)S(1)} fusion(f32[8,128,256]{2,1,0:T(8,128)S(1)} %get-tuple-element.232, s32[32]{0:T(128)S(1)} %get-tuple-element.213, f32[32,128,256]{2,1,0:T(8,128)} %fusion.56), kind=kCustom, calls=%fused_computation.2.clone.1 | custom fusion | flops 1048576 | bytes 12583040 | tf_op jit(solution)/shard_map/while/body/eval_jaxpr/scatter-add | solution.py:39
  203.5 6.4 %scatter_fusion = f32[8,128,256]{2,1,0:T(8,128)S(1)} fusion(f32[8,128,256]{2,1,0:T(8,128)S(1)} %get-tuple-element.232, s32[32]{0:T(128)S(1)} %get-tuple-element.213, f32[32,128,256]{2,1,0:T(8,128)} %fusion.56), kind=kCustom, calls=%fused_computation.2.clone.1 | custom fusion | flops 1048576 | bytes 12583040 | tf_op jit(solution)/shard_map/while/body/eval_jaxpr/scatter-add | solution.py:39
  215.6 6.9 %all-reduce = f32[1024]{0:T(1024)S(1)} all-reduce(f32[1024]{0:T(1024)} %bitcast.96), channel_id=3, replica_groups=mesh['nodes'=8,'cols'=4] {'cols'}, use_global_device_ids=true, to_apply=%region_6.7.clone | all-reduce | flops 1024 | bytes 8192
  222.6 14.7 %reduce-scatter.3.cloned.1.call-done = f32[256,256]{1,0:T(8,128)} async-done(((f32[1024,256]{1,0:T(8,128)}), f32[256,256]{1,0:T(8,128)}) %reduce-scatter.3.cloned.1.call-update) | async-done | bytes 262160 | tf_op jit(solution)/shard_map/reduce_scatter | solution.py:51
  240.5 7.3 %all_gather.7 = bf16[1024,256]{1,0:T(8,128)(2,1)S(1)} all-gather(bf16[256,256]{1,0:T(8,128)(2,1)S(1)} %fusion.28), channel_id=1, replica_groups=mesh['nodes'=8,'cols'=4] {'cols'}, dimensions={0}, use_global_device_ids=true | all-gather | bytes 655360 | tf_op jit(solution)/shard_map/all_gather | solution.py:79
  249.1 160.5 %while.23 = (s32[]{:T(128)}, f32[16,128,256]{2,1,0:T(8,128)S(1)}, s32[11,32]{1,0:T(8,128)}, s32[11,32,16,128]{3,2,1,0:T(8,128)}, s32[11,32]{1,0:T(8,128)S(1)}, /*index=5*/bf16[8,128,256]{2,1,0:T(8,128)(2,1)S(1)}, s32[]{:T(128)}) while((s32[]{:T(128)}, f32[16,128,256]{2,1,0:T(8,128)S(1)}, s32[11,32]{1,0:T(8,128)}, ...), condition=%wide.region_9.10_spmd, body=%wide.region_7.9_spmd.sunk | while | flops 271058112 | bytes 23862236 | solution.py:89
  252.9 4.3 fusion.60
  257.2 6.5 %scatter_fusion.1 = f32[16,128,256]{2,1,0:T(8,128)S(1)} fusion(f32[16,128,256]{2,1,0:T(8,128)S(1)} %get-tuple-element.255, s32[32]{0:T(128)S(1)} %get-tuple-element.221, f32[32,128,256]{2,1,0:T(8,128)} %fusion.60), kind=kCustom, calls=%fused_computation.4.clone.1 | custom fusion | flops 1048576 | bytes 12583040 | tf_op jit(solution)/shard_map/while/body/eval_jaxpr/scatter-add | solution.py:87
  267.5 4.3 fusion.60
  271.8 6.5 %scatter_fusion.1 = f32[16,128,256]{2,1,0:T(8,128)S(1)} fusion(f32[16,128,256]{2,1,0:T(8,128)S(1)} %get-tuple-element.255, s32[32]{0:T(128)S(1)} %get-tuple-element.221, f32[32,128,256]{2,1,0:T(8,128)} %fusion.60), kind=kCustom, calls=%fused_computation.4.clone.1 | custom fusion | flops 1048576 | bytes 12583040 | tf_op jit(solution)/shard_map/while/body/eval_jaxpr/scatter-add | solution.py:87
  282.1 4.3 fusion.60
  286.4 6.5 %scatter_fusion.1 = f32[16,128,256]{2,1,0:T(8,128)S(1)} fusion(f32[16,128,256]{2,1,0:T(8,128)S(1)} %get-tuple-element.255, s32[32]{0:T(128)S(1)} %get-tuple-element.221, f32[32,128,256]{2,1,0:T(8,128)} %fusion.60), kind=kCustom, calls=%fused_computation.4.clone.1 | custom fusion | flops 1048576 | bytes 12583040 | tf_op jit(solution)/shard_map/while/body/eval_jaxpr/scatter-add | solution.py:87
  296.7 4.3 fusion.60
  301.0 6.5 %scatter_fusion.1 = f32[16,128,256]{2,1,0:T(8,128)S(1)} fusion(f32[16,128,256]{2,1,0:T(8,128)S(1)} %get-tuple-element.255, s32[32]{0:T(128)S(1)} %get-tuple-element.221, f32[32,128,256]{2,1,0:T(8,128)} %fusion.60), kind=kCustom, calls=%fused_computation.4.clone.1 | custom fusion | flops 1048576 | bytes 12583040 | tf_op jit(solution)/shard_map/while/body/eval_jaxpr/scatter-add | solution.py:87
  311.3 4.3 fusion.60
  315.6 6.5 %scatter_fusion.1 = f32[16,128,256]{2,1,0:T(8,128)S(1)} fusion(f32[16,128,256]{2,1,0:T(8,128)S(1)} %get-tuple-element.255, s32[32]{0:T(128)S(1)} %get-tuple-element.221, f32[32,128,256]{2,1,0:T(8,128)} %fusion.60), kind=kCustom, calls=%fused_computation.4.clone.1 | custom fusion | flops 1048576 | bytes 12583040 | tf_op jit(solution)/shard_map/while/body/eval_jaxpr/scatter-add | solution.py:87
  325.9 4.3 fusion.60
  330.2 6.5 %scatter_fusion.1 = f32[16,128,256]{2,1,0:T(8,128)S(1)} fusion(f32[16,128,256]{2,1,0:T(8,128)S(1)} %get-tuple-element.255, s32[32]{0:T(128)S(1)} %get-tuple-element.221, f32[32,128,256]{2,1,0:T(8,128)} %fusion.60), kind=kCustom, calls=%fused_computation.4.clone.1 | custom fusion | flops 1048576 | bytes 12583040 | tf_op jit(solution)/shard_map/while/body/eval_jaxpr/scatter-add | solution.py:87
  340.5 4.3 fusion.60
  344.8 6.5 %scatter_fusion.1 = f32[16,128,256]{2,1,0:T(8,128)S(1)} fusion(f32[16,128,256]{2,1,0:T(8,128)S(1)} %get-tuple-element.255, s32[32]{0:T(128)S(1)} %get-tuple-element.221, f32[32,128,256]{2,1,0:T(8,128)} %fusion.60), kind=kCustom, calls=%fused_computation.4.clone.1 | custom fusion | flops 1048576 | bytes 12583040 | tf_op jit(solution)/shard_map/while/body/eval_jaxpr/scatter-add | solution.py:87
  355.1 4.3 fusion.60
  359.4 6.5 %scatter_fusion.1 = f32[16,128,256]{2,1,0:T(8,128)S(1)} fusion(f32[16,128,256]{2,1,0:T(8,128)S(1)} %get-tuple-element.255, s32[32]{0:T(128)S(1)} %get-tuple-element.221, f32[32,128,256]{2,1,0:T(8,128)} %fusion.60), kind=kCustom, calls=%fused_computation.4.clone.1 | custom fusion | flops 1048576 | bytes 12583040 | tf_op jit(solution)/shard_map/while/body/eval_jaxpr/scatter-add | solution.py:87
  369.7 4.3 fusion.60
  374.0 6.5 %scatter_fusion.1 = f32[16,128,256]{2,1,0:T(8,128)S(1)} fusion(f32[16,128,256]{2,1,0:T(8,128)S(1)} %get-tuple-element.255, s32[32]{0:T(128)S(1)} %get-tuple-element.221, f32[32,128,256]{2,1,0:T(8,128)} %fusion.60), kind=kCustom, calls=%fused_computation.4.clone.1 | custom fusion | flops 1048576 | bytes 12583040 | tf_op jit(solution)/shard_map/while/body/eval_jaxpr/scatter-add | solution.py:87
  384.3 4.3 fusion.60
  388.5 6.5 %scatter_fusion.1 = f32[16,128,256]{2,1,0:T(8,128)S(1)} fusion(f32[16,128,256]{2,1,0:T(8,128)S(1)} %get-tuple-element.255, s32[32]{0:T(128)S(1)} %get-tuple-element.221, f32[32,128,256]{2,1,0:T(8,128)} %fusion.60), kind=kCustom, calls=%fused_computation.4.clone.1 | custom fusion | flops 1048576 | bytes 12583040 | tf_op jit(solution)/shard_map/while/body/eval_jaxpr/scatter-add | solution.py:87
  398.8 4.3 fusion.60
  403.1 6.5 %scatter_fusion.1 = f32[16,128,256]{2,1,0:T(8,128)S(1)} fusion(f32[16,128,256]{2,1,0:T(8,128)S(1)} %get-tuple-element.255, s32[32]{0:T(128)S(1)} %get-tuple-element.221, f32[32,128,256]{2,1,0:T(8,128)} %fusion.60), kind=kCustom, calls=%fused_computation.4.clone.1 | custom fusion | flops 1048576 | bytes 12583040 | tf_op jit(solution)/shard_map/while/body/eval_jaxpr/scatter-add | solution.py:87
  411.0 39.4 %psum.23 = f32[256]{0:T(256)} all-reduce(f32[256]{0:T(256)S(1)} %get-tuple-element.128), channel_id=1, replica_groups=mesh['nodes'=8,'cols'=4] {'nodes','cols'}, use_global_device_ids=true, to_apply=%region_14.15 | all-reduce | flops 256 | bytes 2048 | tf_op jit(solution)/shard_map/psum | solution.py:73
  452.2 25.2 %reduce-scatter.5.cloned.1.call-done = f32[256,256]{1,0:T(8,128)} async-done(((f32[2048,256]{1,0:T(8,128)}), f32[256,256]{1,0:T(8,128)}) %reduce-scatter.5.cloned.1.call-update) | async-done | bytes 262160 | tf_op jit(solution)/shard_map/reduce_scatter | solution.py:95
  (240 shorter events, 128.3 us)
Async XLA Ops:
  7.2 230.2 %copy-start = (bf16[256,256]{1,0:T(8,128)(2,1)S(1)}, bf16[256,256]{1,0:T(8,128)(2,1)}, u32[]{:S(2)}) copy-start(bf16[256,256]{1,0:T(8,128)(2,1)} %param.17) | copy-start | bytes 393220
  7.2 44.2 %all-gather.2.cloned.1.call-start = ((), (), s32[]{:S(2)}) async-start(), calls=%async_computation.2 | async-start | bytes 1179648 | tf_op jit(solution)/shard_map/all_gather | solution.py:29
  7.9 229.4 %reduce-scatter.3.cloned.1.call-start = ((), (), s32[]{:S(2)}) async-start(), calls=%async_computation.3 | async-start | bytes 1310720 | tf_op jit(solution)/shard_map/reduce_scatter | solution.py:51
  58.6 6.7 %copy-start.5 = (f32[8,128]{1,0:T(8,128)S(1)}, f32[8,128]{1,0:T(8,128)}, u32[]{:S(2)}) copy-start(f32[8,128]{1,0:T(8,128)} %get-tuple-element.233) | copy-start | bytes 12292 | tf_op jit(solution)/shard_map/while
  66.0 0.6 copy-start.6
  73.0 6.7 %copy-start.5 = (f32[8,128]{1,0:T(8,128)S(1)}, f32[8,128]{1,0:T(8,128)}, u32[]{:S(2)}) copy-start(f32[8,128]{1,0:T(8,128)} %get-tuple-element.233) | copy-start | bytes 12292 | tf_op jit(solution)/shard_map/while
  80.5 0.6 copy-start.6
  87.5 6.7 %copy-start.5 = (f32[8,128]{1,0:T(8,128)S(1)}, f32[8,128]{1,0:T(8,128)}, u32[]{:S(2)}) copy-start(f32[8,128]{1,0:T(8,128)} %get-tuple-element.233) | copy-start | bytes 12292 | tf_op jit(solution)/shard_map/while
  95.0 0.6 copy-start.6
  102.0 6.7 %copy-start.5 = (f32[8,128]{1,0:T(8,128)S(1)}, f32[8,128]{1,0:T(8,128)}, u32[]{:S(2)}) copy-start(f32[8,128]{1,0:T(8,128)} %get-tuple-element.233) | copy-start | bytes 12292 | tf_op jit(solution)/shard_map/while
  109.4 0.6 copy-start.6
  116.5 6.7 %copy-start.5 = (f32[8,128]{1,0:T(8,128)S(1)}, f32[8,128]{1,0:T(8,128)}, u32[]{:S(2)}) copy-start(f32[8,128]{1,0:T(8,128)} %get-tuple-element.233) | copy-start | bytes 12292 | tf_op jit(solution)/shard_map/while
  123.9 0.6 copy-start.6
  131.0 6.7 %copy-start.5 = (f32[8,128]{1,0:T(8,128)S(1)}, f32[8,128]{1,0:T(8,128)}, u32[]{:S(2)}) copy-start(f32[8,128]{1,0:T(8,128)} %get-tuple-element.233) | copy-start | bytes 12292 | tf_op jit(solution)/shard_map/while
  138.4 0.6 copy-start.6
  145.5 6.7 %copy-start.5 = (f32[8,128]{1,0:T(8,128)S(1)}, f32[8,128]{1,0:T(8,128)}, u32[]{:S(2)}) copy-start(f32[8,128]{1,0:T(8,128)} %get-tuple-element.233) | copy-start | bytes 12292 | tf_op jit(solution)/shard_map/while
  152.9 0.6 copy-start.6
  160.0 6.7 %copy-start.5 = (f32[8,128]{1,0:T(8,128)S(1)}, f32[8,128]{1,0:T(8,128)}, u32[]{:S(2)}) copy-start(f32[8,128]{1,0:T(8,128)} %get-tuple-element.233) | copy-start | bytes 12292 | tf_op jit(solution)/shard_map/while
  167.4 0.6 copy-start.6
  174.5 6.7 %copy-start.5 = (f32[8,128]{1,0:T(8,128)S(1)}, f32[8,128]{1,0:T(8,128)}, u32[]{:S(2)}) copy-start(f32[8,128]{1,0:T(8,128)} %get-tuple-element.233) | copy-start | bytes 12292 | tf_op jit(solution)/shard_map/while
  181.9 0.6 copy-start.6
  189.0 6.7 %copy-start.5 = (f32[8,128]{1,0:T(8,128)S(1)}, f32[8,128]{1,0:T(8,128)}, u32[]{:S(2)}) copy-start(f32[8,128]{1,0:T(8,128)} %get-tuple-element.233) | copy-start | bytes 12292 | tf_op jit(solution)/shard_map/while
  196.4 0.6 copy-start.6
  203.5 6.7 %copy-start.5 = (f32[8,128]{1,0:T(8,128)S(1)}, f32[8,128]{1,0:T(8,128)}, u32[]{:S(2)}) copy-start(f32[8,128]{1,0:T(8,128)} %get-tuple-element.233) | copy-start | bytes 12292 | tf_op jit(solution)/shard_map/while
  210.9 0.6 copy-start.6
  211.5 1.0 copy-start.1
  212.5 237.9 %all-reduce.4.cloned.1.call-start = ((), (), s32[]{:S(2)}) async-start(), calls=%async_computation.5 | async-start | bytes 1048576 | tf_op jit(solution)/shard_map/psum | solution.py:73
  214.4 25.2 %copy-start.3 = (bf16[256,256]{1,0:T(8,128)(2,1)S(1)}, bf16[256,256]{1,0:T(8,128)(2,1)}, u32[]{:S(2)}) copy-start(bf16[256,256]{1,0:T(8,128)(2,1)} %param.12) | copy-start | bytes 393220
  237.3 10.5 %copy-start.7 = (f32[256,256]{1,0:T(8,128)S(1)}, f32[256,256]{1,0:T(8,128)}, u32[]{:S(2)}) copy-start(f32[256,256]{1,0:T(8,128)} %reduce-scatter.3.cloned.1.call-done) | copy-start | bytes 786436
  248.9 228.5 %reduce-scatter.5.cloned.1.call-start = ((), (), s32[]{:S(2)}) async-start(), calls=%async_computation.4 | async-start | bytes 2359296 | tf_op jit(solution)/shard_map/reduce_scatter | solution.py:95
  409.6 1.4 copy-start.2
  409.6 67.8 %copy-start.4 = (bf16[256,256]{1,0:T(8,128)(2,1)S(1)}, bf16[256,256]{1,0:T(8,128)(2,1)}, u32[]{:S(2)}) copy-start(bf16[256,256]{1,0:T(8,128)(2,1)} %param.16) | copy-start | bytes 393220
Sparse Core Ops, SparseCore 0:
  10.1 41.2 all-gather.1
  212.6 24.6 reduce-scatter.2
  249.0 127.2 all-reduce.3
  411.1 66.2 reduce-scatter.4
where the time goes:
time: 494 us; the launch traced here: 487 us
  other arithmetic  170 us (34%)
  matrix products  84.9 us (17%)
  waiting for transfers between devices  81.9 us (17%)
  local copies, waits for them, and re-layouts  81.6 us (17%)
  blocking collectives  53.6 us (11%)
  between operations  14.5 us (3%)
    scatter-add x11, other arithmetic, backward_step(): return (src_grad.at[cols_blk].add(products), None)  71.4 us
    scatter-add x11, other arithmetic, forward_step(): summed = summed.at[rows_blk].add(products)  70.8 us
    dot_general x11, matrix products, backward_step(): jnp.einsum('tba,taf->tbf', bits_blk, picked, preferred_element_type=jnp.f...  47.1 us
    all_gather x1, waiting for transfers between devices, shards(): source = lax.all_gather(node_feats, 'nodes', axis=0, tiled=True)  41.3 us
    psum x1, blocking collectives, shards(): lax.psum((self_term, neigh_term, bias_term), ('nodes', 'cols'))  39.4 us
    dot_general x11, matrix products, forward_step(): jnp.einsum('tba,tbf->taf', bits_blk, picked, preferred_element_type=jnp.f...  30.6 us
    reduce_scatter x1, waiting for transfers between devices, shards(): lax.psum_scatter(src_total, 'nodes', scatter_dimension=0, tiled=True)  25.2 us
    shift_right_arithmetic x66, local copies, waits for them, and re-layouts, unpack_tiles(): jnp.right_shift(packed[:, :, None, :], shifts[None, None, :, None]) & 1  23.4 us
  transfers between devices with their start and end apart: 4, of which 3 were waited for; matrix products, arithmetic and copies ran while one was open for 34% of the time, Pallas kernels for 0%

commit v1 on v0

v1 whole, which is shorter than its diff:
```python
import functools

import jax
import jax.numpy as jnp
from jax import lax
from jax.experimental import pallas as pl
from jax.experimental.pallas import tpu as pltpu
from jax.sharding import PartitionSpec as P


def build_kernel(row_ref, col_ref, bits_ref, adj_ref, deg_ref, count_ref):
    source_count, dest_count = count_ref.shape[:2]
    tile_count = bits_ref.shape[0]
    zero = jnp.zeros((4, 16, 128), jnp.int32)

    def clear(s, _):
        for d in range(dest_count):
            count_ref[s, d] = zero
        return 0

    lax.fori_loop(0, source_count, clear, 0)

    def add_tile(t, _):
        r = row_ref[t]
        c = col_ref[t]
        word = bits_ref[t]
        spread = word | (word << 12)
        for j in range(4):
            count_ref[c, r, j] += (spread >> j) & 0x10001
        return 0

    lax.fori_loop(0, tile_count, add_tile, 0, unroll=4)

    deg_ref[...] = jnp.zeros_like(deg_ref)

    def expand(s, _):
        for d in range(dest_count):
            lanes = slice(d * 128, (d + 1) * 128)
            total = jnp.zeros((16, 128), jnp.float32)
            for j in range(4):
                pair = count_ref[s, d, j]
                low = (pair & 0xFFFF).astype(jnp.float32)
                high = (pair >> 16).astype(jnp.float32)
                total = total + (low + high)
                adj_ref[pl.ds(s * 128 + j * 16, 16), lanes] = low.astype(jnp.bfloat16)
                adj_ref[pl.ds(s * 128 + (j + 4) * 16, 16), lanes] = high.astype(jnp.bfloat16)
            deg_ref[:, lanes] += total
        return 0

    lax.fori_loop(0, source_count, expand, 0)


def build(tile_row, tile_col, tile_bits, source_count, dest_count):
    smem = pl.BlockSpec(memory_space=pltpu.SMEM)
    vmem = pl.BlockSpec(memory_space=pltpu.VMEM)
    return pl.pallas_call(
        build_kernel,
        out_shape=(
            jax.ShapeDtypeStruct((source_count * 128, dest_count * 128), jnp.bfloat16),
            jax.ShapeDtypeStruct((16, dest_count * 128), jnp.float32),
        ),
        in_specs=[smem, smem, vmem],
        out_specs=(vmem, vmem),
        scratch_shapes=[pltpu.VMEM((source_count, dest_count, 4, 16, 128), jnp.int32)],
        compiler_params=pltpu.CompilerParams(vmem_limit_bytes=48 * 1024 * 1024),
        cost_estimate=pl.CostEstimate(flops=20_000_000, bytes_accessed=8_000_000, transcendentals=0),
        name="build_adjacency",
    )(tile_row, tile_col, tile_bits)


def transposed(block):
    return block.astype(jnp.float32).T.astype(block.dtype)


def dot(left, right):
    return jnp.dot(left, right, preferred_element_type=jnp.float32)


def dot_nt(left, right):
    return lax.dot_general(left, right, (((1,), (1,)), ((), ())), preferred_element_type=jnp.float32)


def layer_kernel(node_count, col_count, piece, *refs):
    sources = refs[:node_count]
    (adj, deg, feats, w_self, w_neigh, bias, cot) = refs[node_count : node_count + 7]
    (layer_out, feat_grad, self_grad, neigh_grad, bias_grad) = refs[node_count + 7 : node_count + 12]
    (sum_out, sum_in, mean_all, src_out, src_in, part_out, part_in, node_out, node_in, full, sum_send, sum_recv, mean_send, mean_recv, src_send, src_recv, part_send, part_recv,
     node_send, node_recv, piece_send, piece_recv, full_send, full_recv) = refs[node_count + 12 :]
    n = lax.axis_index("nodes")
    c = lax.axis_index("cols")
    rows = feats.shape[0]
    width = feats.shape[1]
    f32, bf16 = jnp.float32, jnp.bfloat16

    def node_at(i):
        return lax.rem(n + i, node_count)

    def col_at(i):
        return lax.rem(c + i, col_count)

    def block(k):
        return pl.ds(pl.multiple_of(k * rows, rows), rows)

    def to_col(src, dst, send, recv, i):
        return pltpu.make_async_remote_copy(
            src_ref=src, dst_ref=dst, send_sem=send, recv_sem=recv,
            device_id=(n, col_at(i)), device_id_type=pl.DeviceIdType.MESH)

    def to_node(src, dst, send, recv, i):
        return pltpu.make_async_remote_copy(
            src_ref=src, dst_ref=dst, send_sem=send, recv_sem=recv,
            device_id=(node_at(i), c), device_id_type=pl.DeviceIdType.MESH)

    barrier = pltpu.get_barrier_semaphore()
    for i in range(1, col_count):
        pl.semaphore_signal(barrier, inc=1, device_id=(n, col_at(i)), device_id_type=pl.DeviceIdType.MESH)
    for i in range(1, node_count):
        pl.semaphore_signal(barrier, inc=1, device_id=(node_at(i), c), device_id_type=pl.DeviceIdType.MESH)
    pl.semaphore_wait(barrier, col_count + node_count - 2)

    def part_sum(col):
        total = jnp.zeros((width, rows), f32)
        for k in range(node_count):
            total = total + dot(sources[k][...], adj[block(lax.rem(n + node_count - k, node_count)), block(col)])
        return total

    def part_degree(col):
        return jnp.sum(deg[:, block(col)], axis=0, keepdims=True)

    def sum_copy(i):
        return to_col(sum_out.at[i - 1], sum_in.at[i - 1], sum_send.at[i - 1], sum_recv.at[i - 1], i)

    first = lax.broadcasted_iota(jnp.int32, (16, rows), 0) == 0

    def send_sum(i, _):
        col = col_at(i)
        sum_out[i - 1, :width] = part_sum(col).astype(bf16)
        degree = part_degree(col)
        high = jnp.floor(degree * (1.0 / 256.0))
        low = degree - high * 256.0
        sum_out[i - 1, width:] = jnp.where(first, high, low).astype(bf16)
        sum_copy(i).start()
        return 0

    lax.fori_loop(1, col_count, send_sum, 0)
    summed = part_sum(c)
    degree = part_degree(c)
    self_act = dot(feats[...], w_self[...]) + bias[...]
    feats_t = transposed(feats[...])
    for i in range(1, col_count):
        sum_copy(i).wait_recv()
        summed = summed + sum_in[i - 1, :width].astype(f32)
        tail = sum_in[i - 1, width:].astype(f32)
        degree = degree + tail[0:1] * 256.0 + tail[1:2]
    degree = jnp.maximum(degree, 1.0)

    mean_t = summed / degree
    mean = mean_t.T.astype(bf16)
    mean_t = mean_t.astype(bf16)
    preact = self_act + dot(mean, w_neigh[...])
    gate = jax.nn.sigmoid(preact)
    layer_out[...] = (preact * gate).astype(bf16)
    pre_grad = (cot[...].astype(f32) * gate * (1.0 + preact * (1.0 - gate))).astype(bf16)
    mean_grad = dot_nt(w_neigh[...], pre_grad) / degree
    mean_all[c] = mean_grad.T.astype(bf16)

    def mean_copy(i):
        return to_col(mean_all.at[c], mean_all.at[c], mean_send.at[i - 1], mean_recv.at[i - 1], i)

    for i in range(1, col_count):
        mean_copy(i).start()

    self_term = dot(feats_t, pre_grad)
    neigh_term = dot(mean_t, pre_grad)
    bias_term = jnp.sum(pre_grad.astype(f32), axis=0, keepdims=True)
    chunk = node_count * piece
    top = lax.broadcasted_iota(jnp.int32, (16, width), 0) == 0

    def split_bias(value):
        high = value.astype(bf16).astype(f32)
        return jnp.where(top, high, value - high).astype(bf16)

    def join_bias(value):
        pair = value.astype(f32)
        return pair[0:1] + pair[1:2]

    terms = jnp.concatenate([self_term, neigh_term], axis=0)
    spare = col_count * chunk - 2 * width
    if spare:
        terms = jnp.concatenate([terms, jnp.zeros((spare, width), f32)], axis=0)
    for k in range(col_count):
        part_out[k, :chunk] = terms[k * chunk : (k + 1) * chunk].astype(bf16)
        part_out[k, chunk:] = split_bias(bias_term)

    def part_copy(i):
        return to_col(part_out.at[col_at(i)], part_in.at[i - 1], part_send.at[i - 1], part_recv.at[i - 1], i)

    for i in range(1, col_count):
        part_copy(i).start()

    self_feat = dot_nt(pre_grad, w_self[...])
    for i in range(1, col_count):
        mean_copy(i).wait_recv()

    def source_part(node):
        total = jnp.zeros((rows, width), f32)
        for k in range(col_count):
            total = total + dot(adj[block(node), k * rows : (k + 1) * rows], mean_all[k])
        return total

    def src_copy(i):
        return to_node(src_out.at[i - 1], src_in.at[i - 1], src_send.at[i - 1], src_recv.at[i - 1], i)

    def send_source(i, _):
        src_out[i - 1] = source_part(node_at(i)).astype(bf16)
        src_copy(i).start()
        return 0

    lax.fori_loop(1, node_count, send_source, 0)

    total = part_out[c, :chunk].astype(f32)
    bias_total = bias_term
    for i in range(1, col_count):
        part_copy(i).wait_recv()
        total = total + part_in[i - 1, :chunk].astype(f32)
        bias_total = bias_total + join_bias(part_in[i - 1, chunk:])
    for k in range(node_count):
        node_out[k, :piece] = total[k * piece : (k + 1) * piece].astype(bf16)
        node_out[k, piece:] = split_bias(bias_total)

    def node_copy(i):
        return to_node(node_out.at[node_at(i)], node_in.at[i - 1], node_send.at[i - 1], node_recv.at[i - 1], i)

    for i in range(1, node_count):
        node_copy(i).start()
    source = source_part(n)
    mine = node_out[n, :piece].astype(f32)
    for i in range(1, node_count):
        node_copy(i).wait_recv()
        mine = mine + node_in[i - 1, :piece].astype(f32)
        bias_total = bias_total + join_bias(node_in[i - 1, piece:])
    bias_grad[...] = bias_total

    own_rows = pl.ds(pl.multiple_of(n * piece, piece), piece)
    full[c, own_rows] = mine.astype(bf16)

    def piece_copy(i):
        return to_node(full.at[c, own_rows], full.at[c, own_rows], piece_send.at[i - 1], piece_recv.at[i - 1], i)

    for i in range(1, node_count):
        piece_copy(i).start()
    for i in range(1, node_count):
        piece_copy(i).wait_recv()

    def full_copy(i):
        return to_col(full.at[c], full.at[c], full_send.at[i - 1], full_recv.at[i - 1], i)

    for i in range(1, col_count):
        full_copy(i).start()

    for i in range(1, node_count):
        src_copy(i).wait_recv()
        source = source + src_in[i - 1].astype(f32)
    to = lax.broadcasted_iota(jnp.int32, (rows, rows), 0)
    frm = lax.broadcasted_iota(jnp.int32, (rows, rows), 1)
    want = (to // 128) * 128 + (to % 8) * 16 + (to % 128) // 8
    order = jnp.where(frm == want, 1.0, 0.0).astype(bf16)
    high = source.astype(bf16)
    low = (source - high.astype(f32)).astype(bf16)
    feat_grad[...] = (self_feat + (dot(order, high) + dot(order, low))).astype(bf16)

    for i in range(1, col_count):
        full_copy(i).wait_recv()
    for k in range(col_count):
        for part in range(chunk // piece):
            row = k * chunk + part * piece
            if row < width:
                self_grad[row : row + piece] = full[k, part * piece : (part + 1) * piece].astype(f32)
            elif row < 2 * width:
                neigh_grad[row - width : row - width + piece] = full[
                    k, part * piece : (part + 1) * piece
                ].astype(f32)
    for i in range(1, col_count):
        sum_copy(i).wait_send()
        mean_copy(i).wait_send()
        part_copy(i).wait_send()
        full_copy(i).wait_send()
    for i in range(1, node_count):
        src_copy(i).wait_send()
        node_copy(i).wait_send()
        piece_copy(i).wait_send()


def layer(sources, adj, deg, feats, w_self, w_neigh, bias, cot, node_count, col_count):
    rows, width = feats.shape
    piece = max(16, 2 * width // (node_count * col_count))
    chunk = node_count * piece
    vmem = pl.BlockSpec(memory_space=pltpu.VMEM)
    bf16, f32 = jnp.bfloat16, jnp.float32
    others, peers = col_count - 1, node_count - 1
    sems = pltpu.SemaphoreType.DMA
    return pl.pallas_call(
        functools.partial(layer_kernel, node_count, col_count, piece),
        out_shape=(
            jax.ShapeDtypeStruct((rows, width), bf16),
            jax.ShapeDtypeStruct((rows, width), bf16),
            jax.ShapeDtypeStruct((width, width), f32),
            jax.ShapeDtypeStruct((width, width), f32),
            jax.ShapeDtypeStruct((1, width), f32),
        ),
        in_specs=[vmem] * (node_count + 7),
        out_specs=(vmem,) * 5,
        scratch_shapes=[
            pltpu.VMEM((others, width + 16, rows), bf16),
            pltpu.VMEM((others, width + 16, rows), bf16),
            pltpu.VMEM((col_count, rows, width), bf16),
            pltpu.VMEM((peers, rows, width), bf16),
            pltpu.VMEM((peers, rows, width), bf16),
            pltpu.VMEM((col_count, chunk + 16, width), bf16),
            pltpu.VMEM((others, chunk + 16, width), bf16),
            pltpu.VMEM((node_count, piece + 16, width), bf16),
            pltpu.VMEM((peers, piece + 16, width), bf16),
            pltpu.VMEM((col_count, chunk, width), bf16),
            sems((others,)), sems((others,)), sems((others,)), sems((others,)),
            sems((peers,)), sems((peers,)), sems((others,)), sems((others,)),
            sems((peers,)), sems((peers,)), sems((peers,)), sems((peers,)),
            sems((others,)), sems((others,)),
        ],
        compiler_params=pltpu.CompilerParams(
            collective_id=0, has_side_effects=True, vmem_limit_bytes=48 * 1024 * 1024
        ),
        cost_estimate=pl.CostEstimate(flops=2_500_000_000, bytes_accessed=9_000_000, transcendentals=70_000),
        name="sage_layer",
    )(*sources, adj, deg, feats, w_self, w_neigh, bias, cot)


def shards(node_feats, tile_row, tile_col, tile_bits, w_self, w_neigh, bias, cotangent):
    rows_dev, width_in = node_feats.shape
    node_count = lax.axis_size("nodes")
    col_count = lax.axis_size("cols")
    per_dev = rows_dev // 128
    ordered = node_feats.reshape(per_dev, 16, 8, width_in).transpose(3, 0, 2, 1).reshape(width_in, rows_dev)
    sources = [ordered]
    for i in range(1, node_count):
        pairs = [(k, (k + i) % node_count) for k in range(node_count)]
        sources.append(lax.ppermute(ordered, "nodes", pairs))
    adj, deg = build(
        tile_row[0], tile_col[0], tile_bits[0], node_count * per_dev, col_count * per_dev
    )
    layer_out, feat_grad, self_grad, neigh_grad, bias_grad = layer(
        sources, adj, deg, node_feats, w_self, w_neigh, bias[None, :], cotangent, node_count, col_count
    )
    return (layer_out, feat_grad, self_grad, neigh_grad, bias_grad[0])


def solution(mesh):
    return jax.shard_map(
        shards,
        mesh=mesh,
        in_specs=(
            P(("nodes", "cols"), None),
            P("nodes", "cols"),
            P("nodes", "cols"),
            P("nodes", "cols", None, None),
            P(),
            P(),
            P(),
            P(("nodes", "cols"), None),
        ),
        out_specs=(P(("nodes", "cols"), None), P(("nodes", "cols"), None), P(), P(), P()),
        check_vma=False,
    )
```

time: 494 us -> 97.8 us (0.20); the launches traced: 487 us -> 97.5 us
  other arithmetic: 170 us -> 1.4 us
  matrix products: 84.9 us -> 0 us
  waiting for transfers between devices: 81.9 us -> 8.8 us
  local copies, waits for them, and re-layouts: 81.6 us -> 10.4 us
  Pallas kernels: 0 us -> 67.2 us
  blocking collectives: 53.6 us -> 0 us
  between operations: 14.5 us -> 0.68 us
  starting transfers between devices: 0.16 us -> 9.03 us
    scatter-add x33 -> x0, other arithmetic: 150 us -> none  [the longest x11 71.4 us: backward_step(): return (src_grad.at[cols_blk].add(products), None)]
    dot_general x28 -> x0, matrix products: 84.9 us -> none  [the longest x11 47.1 us: backward_step(): jnp.einsum('tba,taf->tbf', bits_blk, picked, preferred_element_type=jnp.f...]
    pallas_call x0 -> x2, Pallas kernels: none -> 67.2 us  [the longest x1 60.4 us: layer(): pl.pallas_call(functools.partial(layer_kernel, node_count, col_count, pie...]
    gather x22 -> x0, local copies, waits for them, and re-layouts: 43.1 us -> none  [the longest x11 22.1 us: backward_step(): picked = grad_blocks[rows_blk]]
    all_gather x1 -> x0, waiting for transfers between devices: 41.3 us -> none  [shards(): source = lax.all_gather(node_feats, 'nodes', axis=0, tiled=True)]
    reduce_scatter x2 -> x0, waiting for transfers between devices: 39.9 us -> none  [the longest x1 25.2 us: shards(): lax.psum_scatter(src_total, 'nodes', scatter_dimension=0, tiled=True)]
    psum x1 -> x0, blocking collectives: 39.4 us -> none  [shards(): lax.psum((self_term, neigh_term, bias_term), ('nodes', 'cols'))]
    shift_right_arithmetic x66 -> x0, local copies, waits for them, and re-layouts: 23.4 us -> none  [unpack_tiles(): jnp.right_shift(packed[:, :, None, :], shifts[None, None, :, None]) & 1]
  transfers between devices with their start and end apart: 4 -> 7, of which waited for: 3 -> 3; matrix products, arithmetic and copies ran while one was open for 34% -> 1% of each run, Pallas kernels for 0% -> 7%
where the time goes in v1:
time: 97.8 us; the launch traced here: 97.5 us
  Pallas kernels  67.2 us (69%)
  local copies, waits for them, and re-layouts  10.4 us (11%)
  starting transfers between devices  9.03 us (9%)
  waiting for transfers between devices  8.8 us (9%)
  other arithmetic  1.4 us (1%)
    pallas_call x1, Pallas kernels, layer(): pl.pallas_call(functools.partial(layer_kernel, node_count, col_count, pie...  60.4 us
    unnamed x17, local copies, waits for them, and re-layouts  9.38 us
    ppermute x7, starting transfers between devices, shards(): sources.append(lax.ppermute(ordered, 'nodes', pairs))  9.03 us
    ppermute x7, waiting for transfers between devices, shards(): sources.append(lax.ppermute(ordered, 'nodes', pairs))  8.8 us
    pallas_call x1, Pallas kernels, build(): pl.pallas_call(build_kernel, out_shape=(jax.ShapeDtypeStruct((source_coun...  6.76 us
  transfers between devices with their start and end apart: 7, of which 3 were waited for; matrix products, arithmetic and copies ran while one was open for 1% of the time, Pallas kernels for 7%

profile of v1, /device:TPU:1, one launch (start us, length us, event | category | flops | bytes accessed | tf_op | source)
XLA Modules:
  0.0 97.5 jit_solution(12117864925988811472)
XLA Ops:
  0.6 0.9 copy.22
  1.6 0.1 copy.30.refs_0_
  1.7 5.1 %collective-permute-start.6 = (bf16[256,256]{1,0:T(8,128)(2,1)S(1)}, bf16[256,256]{1,0:T(8,128)(2,1)S(1)}, u32[]{:S(2)}, u32[]{:S(2)}) collective-permute-start(bf16[256,256]{1,0:T(8,128)(2,1)S(1)} %copy.30.refs_0_), channel_id=1, source_target_pairs={{0,28},{4,0},{8,4},{12,8},{16,12},{20,16},{24,20},{28,24},{1,29},{... | collective-permute-start | bytes 393224 | tf_op jit(solution)/shard_map/ppermute | solution.py:346
  6.8 0.2 collective-permute-start.5
  7.0 0.0 collective-permute-start.4
  7.0 2.4 %collective-permute-start.3 = (bf16[256,256]{1,0:T(8,128)(2,1)S(1)}, bf16[256,256]{1,0:T(8,128)(2,1)S(1)}, u32[]{:S(2)}, u32[]{:S(2)}) collective-permute-start(bf16[256,256]{1,0:T(8,128)(2,1)S(1)} %copy.30.refs_0_), channel_id=1, source_target_pairs={{0,16},{4,20},{8,24},{12,28},{16,0},{20,4},{24,8},{28,12},{1,17},{... | collective-permute-start | bytes 393224 | tf_op jit(solution)/shard_map/ppermute | solution.py:346
  9.4 0.0 collective-permute-start.2
  9.4 0.0 collective-permute-done.6.refs_7_
  9.4 1.3 %collective-permute-start.1 = (bf16[256,256]{1,0:T(8,128)(2,1)S(1)}, bf16[256,256]{1,0:T(8,128)(2,1)S(1)}, u32[]{:S(2)}, u32[]{:S(2)}) collective-permute-start(bf16[256,256]{1,0:T(8,128)(2,1)S(1)} %copy.30.refs_0_), channel_id=1, source_target_pairs={{0,8},{4,12},{8,16},{12,20},{16,24},{20,28},{24,0},{28,4},{1,9},{5... | collective-permute-start | bytes 393224 | tf_op jit(solution)/shard_map/ppermute | solution.py:346
  10.7 1.1 %collective-permute-done.5.refs_6_ = bf16[256,256]{1,0:T(8,128)(2,1)S(1)} collective-permute-done((bf16[256,256]{1,0:T(8,128)(2,1)S(1)}, bf16[256,256]{1,0:T(8,128)(2,1)S(1)}, u32[]{:S(2)}, u32[]{:S(2)}) %collective-permute-start.5) | collective-permute-done | bytes 131104 | tf_op jit(solution)/shard_map/ppermute | solution.py:346
  11.8 0.0 collective-permute-start
  11.8 0.7 reduce.row_ref
  12.5 0.7 reduce.1.col_ref
  13.2 0.0 copy-start
  13.2 1.8 %copy-done = s32[1,352,16,128]{3,2,1,0:T(8,128)S(1)} copy-done((s32[1,352,16,128]{3,2,1,0:T(8,128)S(1)}, s32[1,352,16,128]{3,2,1,0:T(8,128)}, u32[]{:S(2)}) %copy-start) | copy-done | bytes 2883608
  15.0 6.8 %build_adjacency.1 = (bf16[2048,1024]{1,0:T(8,128)(2,1)}, f32[16,1024]{1,0:T(8,128)S(1)}) custom-call(s32[352]{0:T(512)S(1)} %reduce.row_ref, s32[352]{0:T(512)S(1)} %reduce.1.col_ref, s32[352,16,128]{2,1,0:T(8,128)S(1)} %bitcast.7), custom_call_target="tpu_custom_call" | custom-call | flops 20000000 | bytes 8000000 | tf_op jit(solution)/shard_map/build_adjacency/pallas_call | solution.py:56
  21.8 0.0 collective-permute-done.4.refs_5_
  21.8 6.7 %collective-permute-done.3.refs_4_ = bf16[256,256]{1,0:T(8,128)(2,1)S(1)} collective-permute-done((bf16[256,256]{1,0:T(8,128)(2,1)S(1)}, bf16[256,256]{1,0:T(8,128)(2,1)S(1)}, u32[]{:S(2)}, u32[]{:S(2)}) %collective-permute-start.3) | collective-permute-done | bytes 131104 | tf_op jit(solution)/shard_map/ppermute | solution.py:346
  28.5 1.0 collective-permute-done.2.refs_3_
  29.5 0.0 collective-permute-done.1.refs_2_
  29.5 0.0 collective-permute-done.refs_1_
  29.5 0.0 copy-start.1
  29.5 0.9 copy-done.1
  30.4 0.0 copy-start.2
  30.4 0.9 copy-done.2
  31.3 0.0 copy-start.3
  31.3 0.9 copy-done.3
  32.2 0.0 copy-start.4
  32.2 0.9 copy-done.4
  33.1 0.0 copy-start.5
  33.1 0.7 copy-done.5
  33.8 60.4 %sage_layer.1 = (bf16[256,256]{1,0:T(8,128)(2,1)S(1)}, bf16[256,256]{1,0:T(8,128)(2,1)S(1)}, f32[256,256]{1,0:T(8,128)S(1)}, f32[256,256]{1,0:T(8,128)S(1)}, f32[1,256]{1,0:T(1,128)S(1)}) custom-call(bf16[256,256]{1,0:T(8,128)(2,1)S(1)} %copy.30.refs_0_, bf16[256,256]{1,0:T(8,128)(2,1)S(1)} %collective-permute-done.refs_1_, ...), custom_call_target="tpu_custom_call" | custom-call | flops 2500000000 | bytes 9000000 | tf_op jit(solution)/shard_map/sage_layer/pallas_call | solution.py:302
  94.2 0.7 copy.36
  94.9 0.7 copy.37
  95.5 0.7 copy.38
  96.2 0.7 copy.39
  96.9 0.6 copy.40
Async XLA Ops:
  1.7 7.8 %collective-permute-start.6 = (bf16[256,256]{1,0:T(8,128)(2,1)S(1)}, bf16[256,256]{1,0:T(8,128)(2,1)S(1)}, u32[]{:S(2)}, u32[]{:S(2)}) collective-permute-start(bf16[256,256]{1,0:T(8,128)(2,1)S(1)} %copy.30.refs_0_), channel_id=1, source_target_pairs={{0,28},{4,0},{8,4},{12,8},{16,12},{20,16},{24,20},{28,24},{1,29},{... | collective-permute-start | bytes 393224 | tf_op jit(solution)/shard_map/ppermute | solution.py:346
  6.8 5.0 %collective-permute-start.5 = (bf16[256,256]{1,0:T(8,128)(2,1)S(1)}, bf16[256,256]{1,0:T(8,128)(2,1)S(1)}, u32[]{:S(2)}, u32[]{:S(2)}) collective-permute-start(bf16[256,256]{1,0:T(8,128)(2,1)S(1)} %copy.30.refs_0_), channel_id=1, source_target_pairs={{0,24},{4,28},{8,0},{12,4},{16,8},{20,12},{24,16},{28,20},{1,25},{... | collective-permute-start | bytes 393224 | tf_op jit(solution)/shard_map/ppermute | solution.py:346
  7.0 14.8 %collective-permute-start.4 = (bf16[256,256]{1,0:T(8,128)(2,1)S(1)}, bf16[256,256]{1,0:T(8,128)(2,1)S(1)}, u32[]{:S(2)}, u32[]{:S(2)}) collective-permute-start(bf16[256,256]{1,0:T(8,128)(2,1)S(1)} %copy.30.refs_0_), channel_id=1, source_target_pairs={{0,20},{4,24},{8,28},{12,0},{16,4},{20,8},{24,12},{28,16},{1,21},{... | collective-permute-start | bytes 393224 | tf_op jit(solution)/shard_map/ppermute | solution.py:346
  7.0 21.5 %collective-permute-start.3 = (bf16[256,256]{1,0:T(8,128)(2,1)S(1)}, bf16[256,256]{1,0:T(8,128)(2,1)S(1)}, u32[]{:S(2)}, u32[]{:S(2)}) collective-permute-start(bf16[256,256]{1,0:T(8,128)(2,1)S(1)} %copy.30.refs_0_), channel_id=1, source_target_pairs={{0,16},{4,20},{8,24},{12,28},{16,0},{20,4},{24,8},{28,12},{1,17},{... | collective-permute-start | bytes 393224 | tf_op jit(solution)/shard_map/ppermute | solution.py:346
  9.4 20.0 %collective-permute-start.2 = (bf16[256,256]{1,0:T(8,128)(2,1)S(1)}, bf16[256,256]{1,0:T(8,128)(2,1)S(1)}, u32[]{:S(2)}, u32[]{:S(2)}) collective-permute-start(bf16[256,256]{1,0:T(8,128)(2,1)S(1)} %copy.30.refs_0_), channel_id=1, source_target_pairs={{0,12},{4,16},{8,20},{12,24},{16,28},{20,0},{24,4},{28,8},{1,13},{... | collective-permute-start | bytes 393224 | tf_op jit(solution)/shard_map/ppermute | solution.py:346
  9.4 20.0 %collective-permute-start.1 = (bf16[256,256]{1,0:T(8,128)(2,1)S(1)}, bf16[256,256]{1,0:T(8,128)(2,1)S(1)}, u32[]{:S(2)}, u32[]{:S(2)}) collective-permute-start(bf16[256,256]{1,0:T(8,128)(2,1)S(1)} %copy.30.refs_0_), channel_id=1, source_target_pairs={{0,8},{4,12},{8,16},{12,20},{16,24},{20,28},{24,0},{28,4},{1,9},{5... | collective-permute-start | bytes 393224 | tf_op jit(solution)/shard_map/ppermute | solution.py:346
  11.8 17.7 %collective-permute-start = (bf16[256,256]{1,0:T(8,128)(2,1)S(1)}, bf16[256,256]{1,0:T(8,128)(2,1)S(1)}, u32[]{:S(2)}, u32[]{:S(2)}) collective-permute-start(bf16[256,256]{1,0:T(8,128)(2,1)S(1)} %copy.30.refs_0_), channel_id=1, source_target_pairs={{0,4},{4,8},{8,12},{12,16},{16,20},{20,24},{24,28},{28,0},{1,5},{5... | collective-permute-start | bytes 393224 | tf_op jit(solution)/shard_map/ppermute | solution.py:346
  13.2 1.8 %copy-start = (s32[1,352,16,128]{3,2,1,0:T(8,128)S(1)}, s32[1,352,16,128]{3,2,1,0:T(8,128)}, u32[]{:S(2)}) copy-start(s32[1,352,16,128]{3,2,1,0:T(8,128)} %param.11) | copy-start | bytes 8650756
  29.5 0.9 copy-start.1
  30.4 0.9 copy-start.2
  31.3 0.9 copy-start.3
  32.2 0.9 copy-start.4
  33.1 0.7 copy-start.5

commit v2 on v1

--- a/solution.py
+++ b/solution.py
@@ -8,9 +8,18 @@
 from jax.sharding import PartitionSpec as P
 
 
-def build_kernel(row_ref, col_ref, bits_ref, adj_ref, deg_ref, count_ref):
+def build_kernel(row_ref, col_ref, bits_hbm, adj_hbm, deg_ref, count_ref, bits_ref, adj_ref, in_sem, out_sem):
     source_count, dest_count = count_ref.shape[:2]
     tile_count = bits_ref.shape[0]
+    batch_count = in_sem.shape[0]
+    batch = tile_count // batch_count
+
+    def load(k):
+        span = pl.ds(k * batch, batch)
+        return pltpu.make_async_copy(bits_hbm.at[0, span], bits_ref.at[span], in_sem.at[k])
+
+    for k in range(batch_count):
+        load(k).start()
     zero = jnp.zeros((4, 16, 128), jnp.int32)
 
     def clear(s, _):
@@ -21,17 +30,23 @@
     lax.fori_loop(0, source_count, clear, 0)
 
     def add_tile(t, _):
-        r = row_ref[t]
-        c = col_ref[t]
+        r = row_ref[0, t]
+        c = col_ref[0, t]
         word = bits_ref[t]
         spread = word | (word << 12)
         for j in range(4):
             count_ref[c, r, j] += (spread >> j) & 0x10001
         return 0
 
-    lax.fori_loop(0, tile_count, add_tile, 0, unroll=4)
+    for k in range(batch_count):
+        load(k).wait()
+        lax.fori_loop(k * batch, (k + 1) * batch, add_tile, 0, unroll=4)
 
     deg_ref[...] = jnp.zeros_like(deg_ref)
+
+    def store(s):
+        span = pl.ds(pl.multiple_of(s * 128, 128), 128)
+        return pltpu.make_async_copy(adj_ref.at[span], adj_hbm.at[span], out_sem.at[s])
 
     def expand(s, _):
         for d in range(dest_count):
@@ -45,24 +60,36 @@
                 adj_ref[pl.ds(s * 128 + j * 16, 16), lanes] = low.astype(jnp.bfloat16)
                 adj_ref[pl.ds(s * 128 + (j + 4) * 16, 16), lanes] = high.astype(jnp.bfloat16)
             deg_ref[:, lanes] += total
+        store(s).start()
         return 0
 
     lax.fori_loop(0, source_count, expand, 0)
+    for s in range(source_count):
+        store(s).wait()
 
 
 def build(tile_row, tile_col, tile_bits, source_count, dest_count):
     smem = pl.BlockSpec(memory_space=pltpu.SMEM)
-    vmem = pl.BlockSpec(memory_space=pltpu.VMEM)
+    hbm = pl.BlockSpec(memory_space=pltpu.HBM)
+    tile_count = tile_row.shape[1]
+    batch_count = 4 if tile_count % 16 == 0 else 1
+    adj_shape = (source_count * 128, dest_count * 128)
     return pl.pallas_call(
         build_kernel,
         out_shape=(
-            jax.ShapeDtypeStruct((source_count * 128, dest_count * 128), jnp.bfloat16),
+            jax.ShapeDtypeStruct(adj_shape, jnp.bfloat16),
             jax.ShapeDtypeStruct((16, dest_count * 128), jnp.float32),
         ),
-        in_specs=[smem, smem, vmem],
-        out_specs=(vmem, vmem),
-        scratch_shapes=[pltpu.VMEM((source_count, dest_count, 4, 16, 128), jnp.int32)],
-        compiler_params=pltpu.CompilerParams(vmem_limit_bytes=48 * 1024 * 1024),
+        in_specs=[smem, smem, hbm],
+        out_specs=(hbm, pl.BlockSpec(memory_space=pltpu.VMEM)),
+        scratch_shapes=[
+            pltpu.VMEM((source_count, dest_count, 4, 16, 128), jnp.int32),
+            pltpu.VMEM((tile_count, 16, 128), jnp.int32),
+            pltpu.VMEM(adj_shape, jnp.bfloat16),
+            pltpu.SemaphoreType.DMA((batch_count,)),
+            pltpu.SemaphoreType.DMA((source_count,)),
+        ],
+        compiler_params=pltpu.CompilerParams(vmem_limit_bytes=63 * 1024 * 1024),
         cost_estimate=pl.CostEstimate(flops=20_000_000, bytes_accessed=8_000_000, transcendentals=0),
         name="build_adjacency",
     )(tile_row, tile_col, tile_bits)
@@ -81,16 +108,29 @@
 
 
 def layer_kernel(node_count, col_count, piece, *refs):
-    sources = refs[:node_count]
-    (adj, deg, feats, w_self, w_neigh, bias, cot) = refs[node_count : node_count + 7]
-    (layer_out, feat_grad, self_grad, neigh_grad, bias_grad) = refs[node_count + 7 : node_count + 12]
-    (sum_out, sum_in, mean_all, src_out, src_in, part_out, part_in, node_out, node_in, full, sum_send, sum_recv, mean_send, mean_recv, src_send, src_recv, part_send, part_recv,
-     node_send, node_recv, piece_send, piece_recv, full_send, full_recv) = refs[node_count + 12 :]
+    hbm_in, outs, scratch = refs[:7], refs[7:12], refs[12:]
+    (layer_out, feat_grad, self_grad, neigh_grad, bias_grad) = outs
+    local, load_sem = scratch[:7], scratch[7]
+    (adj, deg, feats, w_self, w_neigh, bias, cot) = local
+    (blocks, acc, own_source, sum_out, sum_in, mean_all, src_out, src_in, comb_out, comb_in, part_out, part_in,
+     node_out, node_in, full, up_send, down_send, across_send, block_recv, sum_send, sum_recv, mean_send,
+     mean_recv, src_send, src_recv, comb_send, comb_recv, part_send, part_recv,
+     node_send, node_recv, piece_send, piece_recv, full_send, full_recv) = scratch[8:]
     n = lax.axis_index("nodes")
     c = lax.axis_index("cols")
     rows = feats.shape[0]
     width = feats.shape[1]
     f32, bf16 = jnp.float32, jnp.bfloat16
+    length = node_count // 2
+    place = lax.div(n, 2)
+    side = lax.rem(n, 2)
+    partner = place * 2 + 1 - side
+
+    def load(k):
+        return pltpu.make_async_copy(hbm_in[k], local[k], load_sem.at[k])
+
+    for k in (2, 0, 1, 3, 4, 5, 6):
+        load(k).start()
 
     def node_at(i):
         return lax.rem(n + i, node_count)
@@ -111,6 +151,11 @@
             src_ref=src, dst_ref=dst, send_sem=send, recv_sem=recv,
             device_id=(node_at(i), c), device_id_type=pl.DeviceIdType.MESH)
 
+    def to_device(src, dst, send, recv, node):
+        return pltpu.make_async_remote_copy(
+            src_ref=src, dst_ref=dst, send_sem=send, recv_sem=recv,
+            device_id=(node, c), device_id_type=pl.DeviceIdType.MESH)
+
     barrier = pltpu.get_barrier_semaphore()
     for i in range(1, col_count):
         pl.semaphore_signal(barrier, inc=1, device_id=(n, col_at(i)), device_id_type=pl.DeviceIdType.MESH)
@@ -118,11 +163,94 @@
         pl.semaphore_signal(barrier, inc=1, device_id=(node_at(i), c), device_id_type=pl.DeviceIdType.MESH)
     pl.semaphore_wait(barrier, col_count + node_count - 2)
 
+    to = lax.broadcasted_iota(jnp.int32, (rows, rows), 0)
+    frm = lax.broadcasted_iota(jnp.int32, (rows, rows), 1)
+    want = (to // 128) * 128 + (to % 8) * 16 + (to % 128) // 8
+    order = jnp.where(frm == want, 1.0, 0.0).astype(bf16)
+
+    def up(b):
+        return to_device(blocks.at[b], blocks.at[b], up_send.at[b], block_recv.at[b], n + 2)
+
+    def down(b):
+        return to_device(blocks.at[b], blocks.at[b], down_send.at[b], block_recv.at[b], n - 2)
+
+    def across(b):
+        return to_device(blocks.at[b], blocks.at[b], across_send.at[b], block_recv.at[b], partner)
+
+    def accumulate(b):
+        acc[...] += dot(blocks[b], adj[block(b), :])
+
+    load(2).wait()
+    feats_t = transposed(feats[...])
+    blocks[n] = dot(feats_t, order).astype(bf16)
+
+    @pl.when(place + 1 < length)
+    def _():
+        up(n).start()
+
+    @pl.when(place > 0)
+    def _():
+        down(n).start()
+
+    across(n).start()
+    load(0).wait()
+    acc[...] = dot(blocks[n], adj[block(n), :])
+
+    def along(d, _):
+        @pl.when(place - d >= 0)
+        def _():
+            b = n - 2 * d
+            across(b).wait_recv()
+
+            @pl.when(place + 1 < length)
+            def _():
+                up(b).start()
+
+            across(b).start()
+
+        @pl.when(place + d < length)
+        def _():
+            b = n + 2 * d
+            across(b).wait_recv()
+
+            @pl.when(place > 0)
+            def _():
+                down(b).start()
+
+            across(b).start()
+
+        @pl.when(place - d >= 0)
+        def _():
+            accumulate(n - 2 * d)
+
+        @pl.when(place + d < length)
+        def _():
+            accumulate(n + 2 * d)
+
+        return 0
+
+    lax.fori_loop(1, length, along, 0)
+    for k in (1, 3, 4, 5, 6):
+        load(k).wait()
+    self_act = dot(feats[...], w_self[...]) + bias[...]
+
+    def opposite(d, _):
+        @pl.when(place - d >= 0)
+        def _():
+            across(partner - 2 * d).wait_recv()
+            accumulate(partner - 2 * d)
+
+        @pl.when((place + d < length) & (d > 0))
+        def _():
+            across(partner + 2 * d).wait_recv()
+            accumulate(partner + 2 * d)
+
+        return 0
+
+    lax.fori_loop(0, length, opposite, 0)
+
     def part_sum(col):
-        total = jnp.zeros((width, rows), f32)
-        for k in range(node_count):
-            total = total + dot(sources[k][...], adj[block(lax.rem(n + node_count - k, node_count)), block(col)])
-        return total
+        return acc[:, block(col)]
 
     def part_degree(col):
         return jnp.sum(deg[:, block(col)], axis=0, keepdims=True)
@@ -145,8 +273,6 @@
     lax.fori_loop(1, col_count, send_sum, 0)
     summed = part_sum(c)
     degree = part_degree(c)
-    self_act = dot(feats[...], w_self[...]) + bias[...]
-    feats_t = transposed(feats[...])
     for i in range(1, col_count):
         sum_copy(i).wait_recv()
         summed = summed + sum_in[i - 1, :width].astype(f32)
@@ -208,15 +334,21 @@
             total = total + dot(adj[block(node), k * rows : (k + 1) * rows], mean_all[k])
         return total
 
+    def goal(i):
+        return jnp.where(place * 2 < length, length - 1 - i, i)
+
     def src_copy(i):
-        return to_node(src_out.at[i - 1], src_in.at[i - 1], src_send.at[i - 1], src_recv.at[i - 1], i)
+        return to_device(src_out.at[i], src_in.at[i], src_send.at[i], src_recv.at[i], partner)
+
+    def comb_copy(i, sender):
+        return to_device(comb_out.at[i], comb_in.at[sender], comb_send.at[i], comb_recv.at[sender], goal(i) * 2 + side)
 
     def send_source(i, _):
-        src_out[i - 1] = source_part(node_at(i)).astype(bf16)
+        src_out[i] = source_part(goal(i) * 2 + 1 - side).astype(bf16)
         src_copy(i).start()
         return 0
 
-    lax.fori_loop(1, node_count, send_source, 0)
+    lax.fori_loop(0, length, send_source, 0)
 
     total = part_out[c, :chunk].astype(f32)
     bias_total = bias_term
@@ -233,7 +365,24 @@
 
     for i in range(1, node_count):
         node_copy(i).start()
-    source = source_part(n)
+
+    def combine(i, _):
+        part = source_part(goal(i) * 2 + side)
+        src_copy(i).wait_recv()
+        part = part + src_in[i].astype(f32)
+
+        @pl.when(goal(i) != place)
+        def _():
+            comb_out[i] = part.astype(bf16)
+            comb_copy(i, place).start()
+
+        @pl.when(goal(i) == place)
+        def _():
+            own_source[...] = part
+
+        return 0
+
+    lax.fori_loop(0, length, combine, 0)
     mine = node_out[n, :piece].astype(f32)
     for i in range(1, node_count):
         node_copy(i).wait_recv()
@@ -258,13 +407,16 @@
     for i in range(1, col_count):
         full_copy(i).start()
 
-    for i in range(1, node_count):
-        src_copy(i).wait_recv()
-        source = source + src_in[i - 1].astype(f32)
-    to = lax.broadcasted_iota(jnp.int32, (rows, rows), 0)
-    frm = lax.broadcasted_iota(jnp.int32, (rows, rows), 1)
-    want = (to // 128) * 128 + (to % 8) * 16 + (to % 128) // 8
-    order = jnp.where(frm == want, 1.0, 0.0).astype(bf16)
+    def collect(j, _):
+        @pl.when(j != place)
+        def _():
+            comb_copy(0, j).wait_recv()
+            own_source[...] += comb_in[j].astype(f32)
+
+        return 0
+
+    lax.fori_loop(0, length, collect, 0)
+    source = own_source[...]
     high = source.astype(bf16)
     low = (source - high.astype(f32)).astype(bf16)
     feat_grad[...] = (self_feat + (dot(order, high) + dot(order, low))).astype(bf16)
@@ -285,17 +437,39 @@
         mean_copy(i).wait_send()
         part_copy(i).wait_send()
         full_copy(i).wait_send()
+
+    def drain(i, _):
+        src_copy(i).wait_send()
+        across(i * 2 + side).wait_send()
+
+        @pl.when(goal(i) != place)
+        def _():
+            comb_copy(i, place).wait_send()
+
+        @pl.when((i <= place) & (place + 1 < length))
+        def _():
+            up(i * 2 + side).wait_send()
+
+        @pl.when((i >= place) & (place > 0))
+        def _():
+            down(i * 2 + side).wait_send()
+
+        return 0
+
+    lax.fori_loop(0, length, drain, 0)
     for i in range(1, node_count):
-        src_copy(i).wait_send()
         node_copy(i).wait_send()
         piece_copy(i).wait_send()
 
 
-def layer(sources, adj, deg, feats, w_self, w_neigh, bias, cot, node_count, col_count):
+def layer(adj, deg, feats, w_self, w_neigh, bias, cot, node_count, col_count):
     rows, width = feats.shape
     piece = max(16, 2 * width // (node_count * col_count))
     chunk = node_count * piece
     vmem = pl.BlockSpec(memory_space=pltpu.VMEM)
+    hbm = pl.BlockSpec(memory_space=pltpu.HBM)
+    inputs = (adj, deg, feats, w_self, w_neigh, bias, cot)
+    length = node_count // 2
     bf16, f32 = jnp.bfloat16, jnp.float32
     others, peers = col_count - 1, node_count - 1
     sems = pltpu.SemaphoreType.DMA
@@ -308,30 +482,60 @@
             jax.ShapeDtypeStruct((width, width), f32),
             jax.ShapeDtypeStruct((1, width), f32),
         ),
-        in_specs=[vmem] * (node_count + 7),
+        in_specs=[hbm] * 7,
         out_specs=(vmem,) * 5,
         scratch_shapes=[
+            *[pltpu.VMEM(x.shape, x.dtype) for x in inputs],
+            sems((7,)),
+            pltpu.VMEM((node_count, width, rows), bf16),
+            pltpu.VMEM((width, col_count * rows), f32),
+            pltpu.VMEM((rows, width), f32),
             pltpu.VMEM((others, width + 16, rows), bf16),
             pltpu.VMEM((others, width + 16, rows), bf16),
             pltpu.VMEM((col_count, rows, width), bf16),
-            pltpu.VMEM((peers, rows, width), bf16),
-            pltpu.VMEM((peers, rows, width), bf16),
+            pltpu.VMEM((length, rows, width), bf16),
+            pltpu.VMEM((length, rows, width), bf16),
+            pltpu.VMEM((length, rows, width), bf16),
+            pltpu.VMEM((length, rows, width), bf16),
             pltpu.VMEM((col_count, chunk + 16, width), bf16),
             pltpu.VMEM((others, chunk + 16, width), bf16),
             pltpu.VMEM((node_count, piece + 16, width), bf16),
             pltpu.VMEM((peers, piece + 16, width), bf16),
             pltpu.VMEM((col_count, chunk, width), bf16),
+            sems((node_count,)), sems((node_count,)), sems((node_count,)), sems((node_count,)),
             sems((others,)), sems((others,)), sems((others,)), sems((others,)),
-            sems((peers,)), sems((peers,)), sems((others,)), sems((others,)),
+            sems((length,)), sems((length,)), sems((length,)), sems((length,)),
+            sems((others,)), sems((others,)),
             sems((peers,)), sems((peers,)), sems((peers,)), sems((peers,)),
             sems((others,)), sems((others,)),
         ],
         compiler_params=pltpu.CompilerParams(
-            collective_id=0, has_side_effects=True, vmem_limit_bytes=48 * 1024 * 1024
+            collective_id=0, has_side_effects=True, vmem_limit_bytes=63 * 1024 * 1024
         ),
         cost_estimate=pl.CostEstimate(flops=2_500_000_000, bytes_accessed=9_000_000, transcendentals=70_000),
         name="sage_layer",
-    )(*sources, adj, deg, feats, w_self, w_neigh, bias, cot)
+    )(*inputs)
+
+
+def finish_kernel(*refs):
+    copies = [pltpu.make_async_copy(refs[k], refs[5 + k], refs[10].at[k]) for k in range(5)]
+    for copy in copies:
+        copy.start()
+    for copy in copies:
+        copy.wait()
+
+
+def finish(results):
+    hbm = pl.BlockSpec(memory_space=pltpu.HBM)
+    return pl.pallas_call(
+        finish_kernel,
+        out_shape=tuple(jax.ShapeDtypeStruct(x.shape, x.dtype) for x in results),
+        in_specs=[hbm] * 5,
+        out_specs=(hbm,) * 5,
+        scratch_shapes=[pltpu.SemaphoreType.DMA((5,))],
+        compiler_params=pltpu.CompilerParams(vmem_limit_bytes=63 * 1024 * 1024),
+        name="write_results",
+    )(*results)
 
 
 def shards(node_feats, tile_row, tile_col, tile_bits, w_self, w_neigh, bias, cotangent):
@@ -339,16 +543,9 @@
     node_count = lax.axis_size("nodes")
     col_count = lax.axis_size("cols")
     per_dev = rows_dev // 128
-    ordered = node_feats.reshape(per_dev, 16, 8, width_in).transpose(3, 0, 2, 1).reshape(width_in, rows_dev)
-    sources = [ordered]
-    for i in range(1, node_count):
-        pairs = [(k, (k + i) % node_count) for k in range(node_count)]
-        sources.append(lax.ppermute(ordered, "nodes", pairs))
-    adj, deg = build(
-        tile_row[0], tile_col[0], tile_bits[0], node_count * per_dev, col_count * per_dev
-    )
-    layer_out, feat_grad, self_grad, neigh_grad, bias_grad = layer(
-        sources, adj, deg, node_feats, w_self, w_neigh, bias[None, :], cotangent, node_count, col_count
+    adj, deg = build(tile_row, tile_col, tile_bits, node_count * per_dev, col_count * per_dev)
+    layer_out, feat_grad, self_grad, neigh_grad, bias_grad = finish(
+        layer(adj, deg, node_feats, w_self, w_neigh, bias[None, :], cotangent, node_count, col_count)
     )
     return (layer_out, feat_grad, self_grad, neigh_grad, bias_grad[0])
 

time: 97.8 us -> 92.2 us (0.943)
  Pallas kernels: 67.2 us -> 91.4 us
  local copies, waits for them, and re-layouts: 10.4 us -> 0 us
  starting transfers between devices: 9.03 us -> 0 us
  waiting for transfers between devices: 8.8 us -> 0 us
  other arithmetic: 1.4 us -> 0 us
    pallas_call x1 -> x2, Pallas kernels: 6.76 us -> 32 us  [the longest x1 25 us: finish(): pl.pallas_call(finish_kernel, out_shape=tuple((jax.ShapeDtypeStruct(x.sha...]
    unnamed x17 -> x0, local copies, waits for them, and re-layouts: 9.38 us -> none
    ppermute x7 -> x0, starting transfers between devices: 9.03 us -> none  [shards(): sources.append(lax.ppermute(ordered, 'nodes', pairs))]
    ppermute x7 -> x0, waiting for transfers between devices: 8.8 us -> none  [shards(): sources.append(lax.ppermute(ordered, 'nodes', pairs))]
    unnamed x2 -> x0, other arithmetic: 1.4 us -> none
    pallas_call x1, Pallas kernels: 60.4 us -> 59.4 us  [layer(): pl.pallas_call(functools.partial(layer_kernel, node_count, col_count, pie...]
  transfers between devices with their start and end apart: 7 -> 0, of which waited for: 3 -> 0; matrix products, arithmetic and copies ran while one was open for 1% -> 0% of each run, Pallas kernels for 7% -> 0%
where the time goes in v2:
time: 92.2 us; the launch traced here: 92 us
  Pallas kernels  91.4 us (99%)
    pallas_call x1, Pallas kernels, layer(): pl.pallas_call(functools.partial(layer_kernel, node_count, col_count, pie...  59.4 us
    pallas_call x1, Pallas kernels, finish(): pl.pallas_call(finish_kernel, out_shape=tuple((jax.ShapeDtypeStruct(x.sha...  25 us
    pallas_call x1, Pallas kernels, build(): pl.pallas_call(build_kernel, out_shape=(jax.ShapeDtypeStruct(adj_shape, j...  7 us

profile of v2, /device:TPU:1, one launch (start us, length us, event | category | flops | bytes accessed | tf_op | source)
XLA Modules:
  0.0 92.0 jit_solution(3085194635066950395)
XLA Ops:
  0.6 7.0 %build_adjacency.1 = (bf16[2048,1024]{1,0:T(8,128)(2,1)}, f32[16,1024]{1,0:T(8,128)}) custom-call(s32[1,352]{1,0:T(1,128)} %row_ref.1, s32[1,352]{1,0:T(1,128)} %col_ref.1, s32[1,352,16,128]{3,2,1,0:T(8,128)} %bits_hbm.1), custom_call_target="tpu_custom_call" | custom-call | flops 20000000 | bytes 8000000 | tf_op jit(solution)/shard_map/build_adjacency/pallas_call | solution.py:77
  7.6 59.4 %sage_layer.1 = (bf16[256,256]{1,0:T(8,128)(2,1)}, bf16[256,256]{1,0:T(8,128)(2,1)}, f32[256,256]{1,0:T(8,128)}, f32[256,256]{1,0:T(8,128)}, f32[1,256]{1,0:T(1,128)}) custom-call(bf16[2048,1024]{1,0:T(8,128)(2,1)} %get-tuple-element.17.refs_0_, f32[16,1024]{1,0:T(8,128)} %get-tuple-element.18.refs_1_, bf16[256,256]{1,0:T(8,128)(2,1)} %refs_2_.1, ...), custom_call_target="tpu_custom_call" | custom-call | flops 2500000000 | bytes 9000000 | tf_op jit(solution)/shard_map/sage_layer/pallas_call | solution.py:476
  67.0 25.0 %write_results.1 = (bf16[256,256]{1,0:T(8,128)(2,1)}, bf16[256,256]{1,0:T(8,128)(2,1)}, f32[256,256]{1,0:T(8,128)}, f32[256,256]{1,0:T(8,128)}, f32[1,256]{1,0:T(1,128)}) custom-call(bf16[256,256]{1,0:T(8,128)(2,1)} %get-tuple-element.19.refs_0_, bf16[256,256]{1,0:T(8,128)(2,1)} %get-tuple-element.20.refs_1_, f32[256,256]{1,0:T(8,128)} %get-tuple-element.21.refs_2_, ...), custom_call_target="tpu_custom_call" | custom-call | tf_op jit(solution)/shard_map/write_results/pallas_call | solution.py:530

commit v3 on v2

--- a/solution.py
+++ b/solution.py
@@ -112,9 +112,9 @@
     (layer_out, feat_grad, self_grad, neigh_grad, bias_grad) = outs
     local, load_sem = scratch[:7], scratch[7]
     (adj, deg, feats, w_self, w_neigh, bias, cot) = local
-    (blocks, acc, own_source, sum_out, sum_in, mean_all, src_out, src_in, comb_out, comb_in, part_out, part_in,
-     node_out, node_in, full, up_send, down_send, across_send, block_recv, sum_send, sum_recv, mean_send,
-     mean_recv, src_send, src_recv, comb_send, comb_recv, part_send, part_recv,
+    (blocks, acc, own_source, sib_out, sib_in, sum_out, sum_in, mean_all, src_out, src_in, comb_out, comb_in, part_out, part_in,
+     node_out, node_in, full, up_send, down_send, across_send, block_recv, sib_send, sib_recv, sum_send, sum_recv,
+     mean_send, mean_recv, pass_send, src_send, src_recv, comb_send, comb_recv, part_send, part_recv,
      node_send, node_recv, piece_send, piece_recv, full_send, full_recv) = scratch[8:]
     n = lax.axis_index("nodes")
     c = lax.axis_index("cols")
@@ -151,6 +151,23 @@
             src_ref=src, dst_ref=dst, send_sem=send, recv_sem=recv,
             device_id=(node_at(i), c), device_id_type=pl.DeviceIdType.MESH)
 
+    pairs = col_count // 2
+    core = lax.rem(c, 2)
+    line = lax.div(c, 2)
+
+    def col_of(i, k):
+        return lax.rem(line + i, pairs) * 2 + k
+
+    def to_sibling(src, dst, send, recv):
+        return pltpu.make_async_remote_copy(
+            src_ref=src, dst_ref=dst, send_sem=send, recv_sem=recv,
+            device_id=(n, line * 2 + 1 - core), device_id_type=pl.DeviceIdType.MESH)
+
+    def to_peer(src, dst, send, recv, i):
+        return pltpu.make_async_remote_copy(
+            src_ref=src, dst_ref=dst, send_sem=send, recv_sem=recv,
+            device_id=(n, col_of(i, core)), device_id_type=pl.DeviceIdType.MESH)
+
     def to_device(src, dst, send, recv, node):
         return pltpu.make_async_remote_copy(
             src_ref=src, dst_ref=dst, send_sem=send, recv_sem=recv,
@@ -255,29 +272,45 @@
     def part_degree(col):
         return jnp.sum(deg[:, block(col)], axis=0, keepdims=True)
 
+    def sib_copy(i):
+        return to_sibling(sib_out.at[i], sib_in.at[i], sib_send.at[i], sib_recv.at[i])
+
     def sum_copy(i):
-        return to_col(sum_out.at[i - 1], sum_in.at[i - 1], sum_send.at[i - 1], sum_recv.at[i - 1], i)
-
-    first = lax.broadcasted_iota(jnp.int32, (16, rows), 0) == 0
-
-    def send_sum(i, _):
-        col = col_at(i)
-        sum_out[i - 1, :width] = part_sum(col).astype(bf16)
-        degree = part_degree(col)
-        high = jnp.floor(degree * (1.0 / 256.0))
-        low = degree - high * 256.0
-        sum_out[i - 1, width:] = jnp.where(first, high, low).astype(bf16)
+        return to_peer(sum_out.at[i - 1], sum_in.at[i - 1], sum_send.at[i - 1], sum_recv.at[i - 1], i)
+
+    digit = lax.broadcasted_iota(jnp.int32, (16, rows), 0)
+
+    def pack(ref, slot, part, degree):
+        high = jnp.floor(degree * (1.0 / 65536.0))
+        rest = degree - high * 65536.0
+        middle = jnp.floor(rest * (1.0 / 256.0))
+        low = rest - middle * 256.0
+        ref[slot, :width] = part.astype(bf16)
+        ref[slot, width:] = jnp.where(digit == 0, high, jnp.where(digit == 1, middle, low)).astype(bf16)
+
+    def unpack(ref, slot):
+        tail = ref[slot, width:].astype(f32)
+        return ref[slot, :width].astype(f32), tail[0:1] * 65536.0 + tail[1:2] * 256.0 + tail[2:3]
+
+    for i in (*range(1, pairs), 0):
+        col = col_of(i, 1 - core)
+        pack(sib_out, i, part_sum(col), part_degree(col))
+        sib_copy(i).start()
+    for i in range(1, pairs):
+        col = col_of(i, core)
+        sib_copy(i).wait_recv()
+        part, part_deg = unpack(sib_in, i)
+        pack(sum_out, i - 1, part + part_sum(col), part_deg + part_degree(col))
         sum_copy(i).start()
-        return 0
-
-    lax.fori_loop(1, col_count, send_sum, 0)
-    summed = part_sum(c)
-    degree = part_degree(c)
-    for i in range(1, col_count):
+    sib_copy(0).wait_recv()
+    part, part_deg = unpack(sib_in, 0)
+    summed = part + part_sum(c)
+    degree = part_deg + part_degree(c)
+    for i in range(1, pairs):
         sum_copy(i).wait_recv()
-        summed = summed + sum_in[i - 1, :width].astype(f32)
-        tail = sum_in[i - 1, width:].astype(f32)
-        degree = degree + tail[0:1] * 256.0 + tail[1:2]
+        part, part_deg = unpack(sum_in, i - 1)
+        summed = summed + part
+        degree = degree + part_deg
     degree = jnp.maximum(degree, 1.0)
 
     mean_t = summed / degree
@@ -288,13 +321,19 @@
     layer_out[...] = (preact * gate).astype(bf16)
     pre_grad = (cot[...].astype(f32) * gate * (1.0 + preact * (1.0 - gate))).astype(bf16)
     mean_grad = dot_nt(w_neigh[...], pre_grad) / degree
-    mean_all[c] = mean_grad.T.astype(bf16)
-
-    def mean_copy(i):
-        return to_col(mean_all.at[c], mean_all.at[c], mean_send.at[i - 1], mean_recv.at[i - 1], i)
-
-    for i in range(1, col_count):
-        mean_copy(i).start()
+    mean_all[block(c)] = mean_grad.T.astype(bf16)
+
+    def mean_peer(i):
+        held = mean_all.at[block(c)]
+        return to_peer(held, held, mean_send.at[i - 1], mean_recv.at[c], i)
+
+    def mean_sibling(i, k):
+        held = mean_all.at[block(col_of(i, k))]
+        return to_sibling(held, held, pass_send.at[i], mean_recv.at[col_of(i, k)])
+
+    for i in range(1, pairs):
+        mean_peer(i).start()
+    mean_sibling(0, core).start()
 
     self_term = dot(feats_t, pre_grad)
     neigh_term = dot(mean_t, pre_grad)
@@ -325,14 +364,14 @@
         part_copy(i).start()
 
     self_feat = dot_nt(pre_grad, w_self[...])
-    for i in range(1, col_count):
-        mean_copy(i).wait_recv()
+    for i in range(1, pairs):
+        mean_sibling(i, core).wait_recv()
+        mean_sibling(i, core).start()
+    for i in range(pairs):
+        mean_sibling(i, 1 - core).wait_recv()
 
     def source_part(node):
-        total = jnp.zeros((rows, width), f32)
-        for k in range(col_count):
-            total = total + dot(adj[block(node), k * rows : (k + 1) * rows], mean_all[k])
-        return total
+        return dot(adj[block(node), :], mean_all[...])
 
     def goal(i):
         return jnp.where(place * 2 < length, length - 1 - i, i)
@@ -433,10 +472,15 @@
                     k, part * piece : (part + 1) * piece
                 ].astype(f32)
     for i in range(1, col_count):
-        sum_copy(i).wait_send()
-        mean_copy(i).wait_send()
         part_copy(i).wait_send()
         full_copy(i).wait_send()
+
+    for i in range(1, pairs):
+        sum_copy(i).wait_send()
+        mean_peer(i).wait_send()
+    for i in range(pairs):
+        sib_copy(i).wait_send()
+        mean_sibling(i, core).wait_send()
 
     def drain(i, _):
         src_copy(i).wait_send()
@@ -470,6 +514,7 @@
     hbm = pl.BlockSpec(memory_space=pltpu.HBM)
     inputs = (adj, deg, feats, w_self, w_neigh, bias, cot)
     length = node_count // 2
+    pairs = col_count // 2
     bf16, f32 = jnp.bfloat16, jnp.float32
     others, peers = col_count - 1, node_count - 1
     sems = pltpu.SemaphoreType.DMA
@@ -490,9 +535,11 @@
             pltpu.VMEM((node_count, width, rows), bf16),
             pltpu.VMEM((width, col_count * rows), f32),
             pltpu.VMEM((rows, width), f32),
-            pltpu.VMEM((others, width + 16, rows), bf16),
-            pltpu.VMEM((others, width + 16, rows), bf16),
-            pltpu.VMEM((col_count, rows, width), bf16),
+            pltpu.VMEM((pairs, width + 16, rows), bf16),
+            pltpu.VMEM((pairs, width + 16, rows), bf16),
+            pltpu.VMEM((pairs - 1, width + 16, rows), bf16),
+            pltpu.VMEM((pairs - 1, width + 16, rows), bf16),
+            pltpu.VMEM((col_count * rows, width), bf16),
             pltpu.VMEM((length, rows, width), bf16),
             pltpu.VMEM((length, rows, width), bf16),
             pltpu.VMEM((length, rows, width), bf16),
@@ -503,7 +550,8 @@
             pltpu.VMEM((peers, piece + 16, width), bf16),
             pltpu.VMEM((col_count, chunk, width), bf16),
             sems((node_count,)), sems((node_count,)), sems((node_count,)), sems((node_count,)),
-            sems((others,)), sems((others,)), sems((others,)), sems((others,)),
+            sems((pairs,)), sems((pairs,)), sems((pairs - 1,)), sems((pairs - 1,)),
+            sems((pairs - 1,)), sems((col_count,)), sems((pairs,)),
             sems((length,)), sems((length,)), sems((length,)), sems((length,)),
             sems((others,)), sems((others,)),
             sems((peers,)), sems((peers,)), sems((peers,)), sems((peers,)),
@@ -518,11 +566,16 @@
 
 
 def finish_kernel(*refs):
-    copies = [pltpu.make_async_copy(refs[k], refs[5 + k], refs[10].at[k]) for k in range(5)]
-    for copy in copies:
-        copy.start()
-    for copy in copies:
-        copy.wait()
+    given, results, staged, in_sem, out_sem = refs[:5], refs[5:10], refs[10:15], refs[15], refs[16]
+    reads = [pltpu.make_async_copy(given[k], staged[k], in_sem.at[k]) for k in range(5)]
+    writes = [pltpu.make_async_copy(staged[k], results[k], out_sem.at[k]) for k in range(5)]
+    for read in reads:
+        read.start()
+    for read, write in zip(reads, writes):
+        read.wait()
+        write.start()
+    for write in writes:
+        write.wait()
 
 
 def finish(results):
@@ -532,7 +585,11 @@
         out_shape=tuple(jax.ShapeDtypeStruct(x.shape, x.dtype) for x in results),
         in_specs=[hbm] * 5,
         out_specs=(hbm,) * 5,
-        scratch_shapes=[pltpu.SemaphoreType.DMA((5,))],
+        scratch_shapes=[
+            *[pltpu.VMEM(x.shape, x.dtype) for x in results],
+            pltpu.SemaphoreType.DMA((5,)),
+            pltpu.SemaphoreType.DMA((5,)),
+        ],
         compiler_params=pltpu.CompilerParams(vmem_limit_bytes=63 * 1024 * 1024),
         name="write_results",
     )(*results)

time: 92.2 us -> 68.9 us (0.75)
  Pallas kernels: 91.4 us -> 68.1 us
    pallas_call x1, Pallas kernels: 25 us -> 1.96 us  [finish(): pl.pallas_call(finish_kernel, out_shape=tuple((jax.ShapeDtypeStruct(x.sha...]
where the time goes in v3:
time: 68.9 us; the launch traced here: 68.8 us
  Pallas kernels  68.1 us (99%)
    pallas_call x1, Pallas kernels, layer(): pl.pallas_call(functools.partial(layer_kernel, node_count, col_count, pie...  59.1 us
    pallas_call x1, Pallas kernels, build(): pl.pallas_call(build_kernel, out_shape=(jax.ShapeDtypeStruct(adj_shape, j...  7 us
    pallas_call x1, Pallas kernels, finish(): pl.pallas_call(finish_kernel, out_shape=tuple((jax.ShapeDtypeStruct(x.sha...  1.96 us

profile of v3, /device:TPU:1, one launch (start us, length us, event | category | flops | bytes accessed | tf_op | source)
XLA Modules:
  0.0 68.8 jit_solution(5830902744460467795)
XLA Ops:
  0.6 7.0 %build_adjacency.1 = (bf16[2048,1024]{1,0:T(8,128)(2,1)}, f32[16,1024]{1,0:T(8,128)}) custom-call(s32[1,352]{1,0:T(1,128)} %row_ref.1, s32[1,352]{1,0:T(1,128)} %col_ref.1, s32[1,352,16,128]{3,2,1,0:T(8,128)} %bits_hbm.1), custom_call_target="tpu_custom_call" | custom-call | flops 20000000 | bytes 8000000 | tf_op jit(solution)/shard_map/build_adjacency/pallas_call | solution.py:77
  7.6 59.1 %sage_layer.1 = (bf16[256,256]{1,0:T(8,128)(2,1)}, bf16[256,256]{1,0:T(8,128)(2,1)}, f32[256,256]{1,0:T(8,128)}, f32[256,256]{1,0:T(8,128)}, f32[1,256]{1,0:T(1,128)}) custom-call(bf16[2048,1024]{1,0:T(8,128)(2,1)} %get-tuple-element.17.refs_0_, f32[16,1024]{1,0:T(8,128)} %get-tuple-element.18.refs_1_, bf16[256,256]{1,0:T(8,128)(2,1)} %refs_2_.1, ...), custom_call_target="tpu_custom_call" | custom-call | flops 2500000000 | bytes 9000000 | tf_op jit(solution)/shard_map/sage_layer/pallas_call | solution.py:521
  66.8 2.0 %write_results.1 = (bf16[256,256]{1,0:T(8,128)(2,1)}, bf16[256,256]{1,0:T(8,128)(2,1)}, f32[256,256]{1,0:T(8,128)}, f32[256,256]{1,0:T(8,128)}, f32[1,256]{1,0:T(1,128)}) custom-call(bf16[256,256]{1,0:T(8,128)(2,1)} %get-tuple-element.19.refs_0_, bf16[256,256]{1,0:T(8,128)(2,1)} %get-tuple-element.20.refs_1_, f32[256,256]{1,0:T(8,128)} %get-tuple-element.21.refs_2_, ...), custom_call_target="tpu_custom_call" | custom-call | tf_op jit(solution)/shard_map/write_results/pallas_call | solution.py:583

commit v4 on v3

--- a/solution.py
+++ b/solution.py
@@ -34,8 +34,9 @@
         c = col_ref[0, t]
         word = bits_ref[t]
         spread = word | (word << 12)
+        sums = [count_ref[c, r, j] + ((spread >> j) & 0x10001) for j in range(4)]
         for j in range(4):
-            count_ref[c, r, j] += (spread >> j) & 0x10001
+            count_ref[c, r, j] = sums[j]
         return 0
 
     for k in range(batch_count):
@@ -338,6 +339,7 @@
     self_term = dot(feats_t, pre_grad)
     neigh_term = dot(mean_t, pre_grad)
     bias_term = jnp.sum(pre_grad.astype(f32), axis=0, keepdims=True)
+    group = col_count * piece
     chunk = node_count * piece
     top = lax.broadcasted_iota(jnp.int32, (16, width), 0) == 0
 
@@ -350,18 +352,18 @@
         return pair[0:1] + pair[1:2]
 
     terms = jnp.concatenate([self_term, neigh_term], axis=0)
-    spare = col_count * chunk - 2 * width
+    spare = node_count * group - 2 * width
     if spare:
         terms = jnp.concatenate([terms, jnp.zeros((spare, width), f32)], axis=0)
-    for k in range(col_count):
-        part_out[k, :chunk] = terms[k * chunk : (k + 1) * chunk].astype(bf16)
-        part_out[k, chunk:] = split_bias(bias_term)
-
-    def part_copy(i):
-        return to_col(part_out.at[col_at(i)], part_in.at[i - 1], part_send.at[i - 1], part_recv.at[i - 1], i)
-
-    for i in range(1, col_count):
-        part_copy(i).start()
+    for k in range(node_count):
+        node_out[k, :group] = terms[k * group : (k + 1) * group].astype(bf16)
+        node_out[k, group:] = split_bias(bias_term)
+
+    def node_copy(i):
+        return to_node(node_out.at[node_at(i)], node_in.at[i - 1], node_send.at[i - 1], node_recv.at[i - 1], i)
+
+    for i in range(1, node_count):
+        node_copy(i).start()
 
     self_feat = dot_nt(pre_grad, w_self[...])
     for i in range(1, pairs):
@@ -389,21 +391,21 @@
 
     lax.fori_loop(0, length, send_source, 0)
 
-    total = part_out[c, :chunk].astype(f32)
+    total = node_out[n, :group].astype(f32)
     bias_total = bias_term
+    for i in range(1, node_count):
+        node_copy(i).wait_recv()
+        total = total + node_in[i - 1, :group].astype(f32)
+        bias_total = bias_total + join_bias(node_in[i - 1, group:])
+    for k in range(col_count):
+        part_out[k, :piece] = total[k * piece : (k + 1) * piece].astype(bf16)
+        part_out[k, piece:] = split_bias(bias_total)
+
+    def part_copy(i):
+        return to_col(part_out.at[col_at(i)], part_in.at[i - 1], part_send.at[i - 1], part_recv.at[i - 1], i)
+
     for i in range(1, col_count):
-        part_copy(i).wait_recv()
-        total = total + part_in[i - 1, :chunk].astype(f32)
-        bias_total = bias_total + join_bias(part_in[i - 1, chunk:])
-    for k in range(node_count):
-        node_out[k, :piece] = total[k * piece : (k + 1) * piece].astype(bf16)
-        node_out[k, piece:] = split_bias(bias_total)
-
-    def node_copy(i):
-        return to_node(node_out.at[node_at(i)], node_in.at[i - 1], node_send.at[i - 1], node_recv.at[i - 1], i)
-
-    for i in range(1, node_count):
-        node_copy(i).start()
+        part_copy(i).start()
 
     def combine(i, _):
         part = source_part(goal(i) * 2 + side)
@@ -421,12 +423,12 @@
 
         return 0
 
-    lax.fori_loop(0, length, combine, 0)
-    mine = node_out[n, :piece].astype(f32)
-    for i in range(1, node_count):
-        node_copy(i).wait_recv()
-        mine = mine + node_in[i - 1, :piece].astype(f32)
-        bias_total = bias_total + join_bias(node_in[i - 1, piece:])
+    lax.fori_loop(0, 1, combine, 0)
+    mine = part_out[c, :piece].astype(f32)
+    for i in range(1, col_count):
+        part_copy(i).wait_recv()
+        mine = mine + part_in[i - 1, :piece].astype(f32)
+        bias_total = bias_total + join_bias(part_in[i - 1, piece:])
     bias_grad[...] = bias_total
 
     own_rows = pl.ds(pl.multiple_of(n * piece, piece), piece)
@@ -437,6 +439,7 @@
 
     for i in range(1, node_count):
         piece_copy(i).start()
+    lax.fori_loop(1, length, combine, 0)
     for i in range(1, node_count):
         piece_copy(i).wait_recv()
 
@@ -464,7 +467,7 @@
         full_copy(i).wait_recv()
     for k in range(col_count):
         for part in range(chunk // piece):
-            row = k * chunk + part * piece
+            row = (part * col_count + k) * piece
             if row < width:
                 self_grad[row : row + piece] = full[k, part * piece : (part + 1) * piece].astype(f32)
             elif row < 2 * width:
@@ -509,6 +512,7 @@
 def layer(adj, deg, feats, w_self, w_neigh, bias, cot, node_count, col_count):
     rows, width = feats.shape
     piece = max(16, 2 * width // (node_count * col_count))
+    group = col_count * piece
     chunk = node_count * piece
     vmem = pl.BlockSpec(memory_space=pltpu.VMEM)
     hbm = pl.BlockSpec(memory_space=pltpu.HBM)
@@ -544,10 +548,10 @@
             pltpu.VMEM((length, rows, width), bf16),
             pltpu.VMEM((length, rows, width), bf16),
             pltpu.VMEM((length, rows, width), bf16),
-            pltpu.VMEM((col_count, chunk + 16, width), bf16),
-            pltpu.VMEM((others, chunk + 16, width), bf16),
-            pltpu.VMEM((node_count, piece + 16, width), bf16),
-            pltpu.VMEM((peers, piece + 16, width), bf16),
+            pltpu.VMEM((col_count, piece + 16, width), bf16),
+            pltpu.VMEM((others, piece + 16, width), bf16),
+            pltpu.VMEM((node_count, group + 16, width), bf16),
+            pltpu.VMEM((peers, group + 16, width), bf16),
             pltpu.VMEM((col_count, chunk, width), bf16),
             sems((node_count,)), sems((node_count,)), sems((node_count,)), sems((node_count,)),
             sems((pairs,)), sems((pairs,)), sems((pairs - 1,)), sems((pairs - 1,)),

time: 68.9 us -> 66.7 us (0.968)
  Pallas kernels: 68.1 us -> 65.9 us
    pallas_call x1, Pallas kernels: 59.1 us -> 56.9 us  [layer(): pl.pallas_call(functools.partial(layer_kernel, node_count, col_count, pie...]
where the time goes in v4:
time: 66.7 us; the launch traced here: 66.6 us
  Pallas kernels  65.9 us (99%)
    pallas_call x1, Pallas kernels, layer(): pl.pallas_call(functools.partial(layer_kernel, node_count, col_count, pie...  56.9 us
    pallas_call x1, Pallas kernels, build(): pl.pallas_call(build_kernel, out_shape=(jax.ShapeDtypeStruct(adj_shape, j...  7 us
    pallas_call x1, Pallas kernels, finish(): pl.pallas_call(finish_kernel, out_shape=tuple((jax.ShapeDtypeStruct(x.sha...  1.96 us

profile of v4, /device:TPU:1, one launch (start us, length us, event | category | flops | bytes accessed | tf_op | source)
XLA Modules:
  0.0 66.6 jit_solution(16482462199214008642)
XLA Ops:
  0.6 7.0 %build_adjacency.1 = (bf16[2048,1024]{1,0:T(8,128)(2,1)}, f32[16,1024]{1,0:T(8,128)}) custom-call(s32[1,352]{1,0:T(1,128)} %row_ref.1, s32[1,352]{1,0:T(1,128)} %col_ref.1, s32[1,352,16,128]{3,2,1,0:T(8,128)} %bits_hbm.1), custom_call_target="tpu_custom_call" | custom-call | flops 20000000 | bytes 8000000 | tf_op jit(solution)/shard_map/build_adjacency/pallas_call | solution.py:78
  7.6 56.9 %sage_layer.1 = (bf16[256,256]{1,0:T(8,128)(2,1)}, bf16[256,256]{1,0:T(8,128)(2,1)}, f32[256,256]{1,0:T(8,128)}, f32[256,256]{1,0:T(8,128)}, f32[1,256]{1,0:T(1,128)}) custom-call(bf16[2048,1024]{1,0:T(8,128)(2,1)} %get-tuple-element.17.refs_0_, f32[16,1024]{1,0:T(8,128)} %get-tuple-element.18.refs_1_, bf16[256,256]{1,0:T(8,128)(2,1)} %refs_2_.1, ...), custom_call_target="tpu_custom_call" | custom-call | flops 2500000000 | bytes 9000000 | tf_op jit(solution)/shard_map/sage_layer/pallas_call | solution.py:525
  64.6 2.0 %write_results.1 = (bf16[256,256]{1,0:T(8,128)(2,1)}, bf16[256,256]{1,0:T(8,128)(2,1)}, f32[256,256]{1,0:T(8,128)}, f32[256,256]{1,0:T(8,128)}, f32[1,256]{1,0:T(1,128)}) custom-call(bf16[256,256]{1,0:T(8,128)(2,1)} %get-tuple-element.19.refs_0_, bf16[256,256]{1,0:T(8,128)(2,1)} %get-tuple-element.20.refs_1_, f32[256,256]{1,0:T(8,128)} %get-tuple-element.21.refs_2_, ...), custom_call_target="tpu_custom_call" | custom-call | tf_op jit(solution)/shard_map/write_results/pallas_call | solution.py:587

commit v5 on v4

--- a/solution.py
+++ b/solution.py
@@ -8,7 +8,7 @@
 from jax.sharding import PartitionSpec as P
 
 
-def build_kernel(row_ref, col_ref, bits_hbm, adj_hbm, deg_ref, count_ref, bits_ref, adj_ref, in_sem, out_sem):
+def build_kernel(row_ref, col_ref, bits_hbm, adj_hbm, deg_ref, count_ref, other_ref, bits_ref, adj_ref, in_sem, out_sem):
     source_count, dest_count = count_ref.shape[:2]
     tile_count = bits_ref.shape[0]
     batch_count = in_sem.shape[0]
@@ -25,23 +25,29 @@
     def clear(s, _):
         for d in range(dest_count):
             count_ref[s, d] = zero
+            other_ref[s, d] = zero
         return 0
 
     lax.fori_loop(0, source_count, clear, 0)
 
-    def add_tile(t, _):
-        r = row_ref[0, t]
-        c = col_ref[0, t]
-        word = bits_ref[t]
-        spread = word | (word << 12)
-        sums = [count_ref[c, r, j] + ((spread >> j) & 0x10001) for j in range(4)]
-        for j in range(4):
-            count_ref[c, r, j] = sums[j]
+    half = batch // 2
+
+    def add_tiles(t, _):
+        pending = []
+        for counts, at in ((count_ref, t), (other_ref, t + half)):
+            r = row_ref[0, at]
+            c = col_ref[0, at]
+            word = bits_ref[at]
+            spread = word | (word << 12)
+            pending.append((counts, r, c, [counts[c, r, j] + ((spread >> j) & 0x10001) for j in range(4)]))
+        for counts, r, c, sums in pending:
+            for j in range(4):
+                counts[c, r, j] = sums[j]
         return 0
 
     for k in range(batch_count):
         load(k).wait()
-        lax.fori_loop(k * batch, (k + 1) * batch, add_tile, 0, unroll=4)
+        lax.fori_loop(k * batch, k * batch + half, add_tiles, 0, unroll=4)
 
     deg_ref[...] = jnp.zeros_like(deg_ref)
 
@@ -54,7 +60,7 @@
             lanes = slice(d * 128, (d + 1) * 128)
             total = jnp.zeros((16, 128), jnp.float32)
             for j in range(4):
-                pair = count_ref[s, d, j]
+                pair = count_ref[s, d, j] + other_ref[s, d, j]
                 low = (pair & 0xFFFF).astype(jnp.float32)
                 high = (pair >> 16).astype(jnp.float32)
                 total = total + (low + high)
@@ -84,6 +90,7 @@
         in_specs=[smem, smem, hbm],
         out_specs=(hbm, pl.BlockSpec(memory_space=pltpu.VMEM)),
         scratch_shapes=[
+            pltpu.VMEM((source_count, dest_count, 4, 16, 128), jnp.int32),
             pltpu.VMEM((source_count, dest_count, 4, 16, 128), jnp.int32),
             pltpu.VMEM((tile_count, 16, 128), jnp.int32),
             pltpu.VMEM(adj_shape, jnp.bfloat16),
@@ -391,6 +398,23 @@
 
     lax.fori_loop(0, length, send_source, 0)
 
+    def combine(i, _):
+        part = source_part(goal(i) * 2 + side)
+        src_copy(i).wait_recv()
+        part = part + src_in[i].astype(f32)
+
+        @pl.when(goal(i) != place)
+        def _():
+            comb_out[i] = part.astype(bf16)
+            comb_copy(i, place).start()
+
+        @pl.when(goal(i) == place)
+        def _():
+            own_source[...] = part
+
+        return 0
+
+    lax.fori_loop(0, 1, combine, 0)
     total = node_out[n, :group].astype(f32)
     bias_total = bias_term
     for i in range(1, node_count):
@@ -407,23 +431,7 @@
     for i in range(1, col_count):
         part_copy(i).start()
 
-    def combine(i, _):
-        part = source_part(goal(i) * 2 + side)
-        src_copy(i).wait_recv()
-        part = part + src_in[i].astype(f32)
-
-        @pl.when(goal(i) != place)
-        def _():
-            comb_out[i] = part.astype(bf16)
-            comb_copy(i, place).start()
-
-        @pl.when(goal(i) == place)
-        def _():
-            own_source[...] = part
-
-        return 0
-
-    lax.fori_loop(0, 1, combine, 0)
+    lax.fori_loop(1, 2, combine, 0)
     mine = part_out[c, :piece].astype(f32)
     for i in range(1, col_count):
         part_copy(i).wait_recv()
@@ -439,7 +447,7 @@
 
     for i in range(1, node_count):
         piece_copy(i).start()
-    lax.fori_loop(1, length, combine, 0)
+    lax.fori_loop(2, length, combine, 0)
     for i in range(1, node_count):
         piece_copy(i).wait_recv()
 

time: 66.7 us -> 69 us (1.034)
  Pallas kernels: 65.9 us -> 68.1 us
    pallas_call x1, Pallas kernels: 56.9 us -> 59.6 us  [layer(): pl.pallas_call(functools.partial(layer_kernel, node_count, col_count, pie...]
where the time goes in v5:
time: 69 us; the launch traced here: 68.8 us
  Pallas kernels  68.1 us (99%)
    pallas_call x1, Pallas kernels, layer(): pl.pallas_call(functools.partial(layer_kernel, node_count, col_count, pie...  59.6 us
    pallas_call x1, Pallas kernels, build(): pl.pallas_call(build_kernel, out_shape=(jax.ShapeDtypeStruct(adj_shape, j...  6.52 us
    pallas_call x1, Pallas kernels, finish(): pl.pallas_call(finish_kernel, out_shape=tuple((jax.ShapeDtypeStruct(x.sha...  1.96 us

profile of v5, /device:TPU:1, one launch (start us, length us, event | category | flops | bytes accessed | tf_op | source)
XLA Modules:
  0.0 68.8 jit_solution(8165383039593878600)
XLA Ops:
  0.6 6.5 %build_adjacency.1 = (bf16[2048,1024]{1,0:T(8,128)(2,1)}, f32[16,1024]{1,0:T(8,128)}) custom-call(s32[1,352]{1,0:T(1,128)} %row_ref.1, s32[1,352]{1,0:T(1,128)} %col_ref.1, s32[1,352,16,128]{3,2,1,0:T(8,128)} %bits_hbm.1), custom_call_target="tpu_custom_call" | custom-call | flops 20000000 | bytes 8000000 | tf_op jit(solution)/shard_map/build_adjacency/pallas_call | solution.py:84
  7.2 59.6 %sage_layer.1 = (bf16[256,256]{1,0:T(8,128)(2,1)}, bf16[256,256]{1,0:T(8,128)(2,1)}, f32[256,256]{1,0:T(8,128)}, f32[256,256]{1,0:T(8,128)}, f32[1,256]{1,0:T(1,128)}) custom-call(bf16[2048,1024]{1,0:T(8,128)(2,1)} %get-tuple-element.17.refs_0_, f32[16,1024]{1,0:T(8,128)} %get-tuple-element.18.refs_1_, bf16[256,256]{1,0:T(8,128)(2,1)} %refs_2_.1, ...), custom_call_target="tpu_custom_call" | custom-call | flops 2500000000 | bytes 9000000 | tf_op jit(solution)/shard_map/sage_layer/pallas_call | solution.py:533
  66.8 2.0 %write_results.1 = (bf16[256,256]{1,0:T(8,128)(2,1)}, bf16[256,256]{1,0:T(8,128)(2,1)}, f32[256,256]{1,0:T(8,128)}, f32[256,256]{1,0:T(8,128)}, f32[1,256]{1,0:T(1,128)}) custom-call(bf16[256,256]{1,0:T(8,128)(2,1)} %get-tuple-element.19.refs_0_, bf16[256,256]{1,0:T(8,128)(2,1)} %get-tuple-element.20.refs_1_, f32[256,256]{1,0:T(8,128)} %get-tuple-element.21.refs_2_, ...), custom_call_target="tpu_custom_call" | custom-call | tf_op jit(solution)/shard_map/write_results/pallas_call | solution.py:595
